TPU v7x, 128 devices: a whole 4x4x4 slice. The times are simulated.
128 devices in a mesh: row: 8 (over y, core), col: 16 (over z, x).
Axes of the slice: x: 4, y: 4, z: 4, core: 2. Of those that a mesh axis runs over, the one named last changes fastest.
Arguments:
- inputs: bfloat16 [1280, 6144], P('col', 'row'), may hold values from -6 to 6
- w_in: bfloat16 [6144, 24576], P('row', 'col'), may hold values from -0.078125 to 0.078125
- b_in: float32 [24576], P('col'), may hold values from -3 to 3
- w_out: bfloat16 [24576, 6144], P('col', 'row'), may hold values from -0.0390625 to 0.0390625
- b_out: float32 [6144], P('row'), may hold values from -3 to 3
- out_grad: bfloat16 [1280, 6144], P('col', 'row'), may hold values from -0.625 to 0.625
Outputs:
- output: bfloat16 [1280, 6144], P('col', 'row')
- input_grad: bfloat16 [1280, 6144], P('col', 'row')
- w_in_grad: float32 [6144, 24576], P('row', 'col')
- b_in_grad: float32 [24576], P('col')
- w_out_grad: float32 [24576, 6144], P('col', 'row')
- b_out_grad: float32 [6144], P('row')
All inputs are finite; a program needn't handle non-finite values.
Results may differ from a plain program's by a relative error of at most 0.007.
Values may be sent and summed in bfloat16 or wider, within the bound.
A program may use at most 128 MiB of HBM per device.

v0:
```python
import jax
import jax.numpy as jnp
from jax import lax
from jax.sharding import PartitionSpec as P


def gelu_parts(hidden):
    half = 0.5 * (1.0 + jax.scipy.special.erf(hidden * 0.7071067811865476))
    slope = half + hidden * jnp.exp(-0.5 * hidden * hidden) * 0.3989422804014327
    return (hidden * half, slope)


def shards(inputs, w_in, b_in, w_out, b_out, out_grad):
    inputs_all, grad_all = (
        lax.all_gather(inputs, "col", axis=0, tiled=True),
        lax.all_gather(out_grad, "col", axis=0, tiled=True),
    )
    partial_value = jnp.dot(inputs_all, w_in, preferred_element_type=jnp.float32)
    hidden = lax.psum(partial_value, "row") + b_in
    act, slope = gelu_parts(hidden)
    act_all = act.astype(jnp.bfloat16)
    rows = act_all
    output = (
        lax.psum_scatter(
            jnp.dot(rows, w_out, preferred_element_type=jnp.float32),
            "col",
            scatter_dimension=0,
            tiled=True,
        )
        + b_out
    ).astype(jnp.bfloat16)
    b_out_grad = jnp.sum(grad_all, axis=0, dtype=jnp.float32)
    w_out_grad = jnp.einsum("tf,td->fd", act_all, grad_all, preferred_element_type=jnp.float32)
    partial_grad = jnp.einsum("td,fd->tf", grad_all, w_out, preferred_element_type=jnp.float32)
    act_grad = lax.psum(partial_grad, "row")
    pre_grad = (act_grad * slope).astype(jnp.bfloat16)
    b_in_grad = jnp.sum(pre_grad, axis=0, dtype=jnp.float32)
    w_in_grad = jnp.einsum("td,tf->df", inputs_all, pre_grad, preferred_element_type=jnp.float32)
    rows = pre_grad
    input_grad = lax.psum_scatter(
        jnp.einsum("tf,df->td", rows, w_in, preferred_element_type=jnp.float32),
        "col",
        scatter_dimension=0,
        tiled=True,
    ).astype(jnp.bfloat16)
    return (output, input_grad, w_in_grad, b_in_grad, w_out_grad, b_out_grad)


def solution(mesh):
    placed = (
        P("col", "row"),
        P("row", "col"),
        P("col"),
        P("col", "row"),
        P("row"),
        P("col", "row"),
    )
    return jax.shard_map(
        shards,
        mesh=mesh,
        in_specs=placed,
        out_specs=(
            P("col", "row"),
            P("col", "row"),
            P("row", "col"),
            P("col"),
            P("col", "row"),
            P("row"),
        ),
        check_vma=False,
    )
```

profile of v0, /device:TPU:0, one launch (start us, length us, event | category | flops | bytes accessed | tf_op | source)
XLA Modules:
  0.0 465.8 jit_solution(393771307948937727)
XLA Ops:
  7.2 0.0 copy-start
  7.2 0.0 all-gather.5.cloned.1.call-start
  7.2 0.7 all-gather.5.cloned.1.call-update
  7.9 0.0 all-gather.3.cloned.1.call-start
  8.0 0.7 all-gather.3.cloned.1.call-update
  8.7 0.0 all-reduce.3.cloned.1.call-start
  8.7 48.7 %all-gather.5.cloned.1.call-done = bf16[1280,768]{1,0:T(8,128)(2,1)} async-done(((bf16[80,768]{1,0:T(8,128)(2,1)}), bf16[1280,768]{1,0:T(8,128)(2,1)}) %all-gather.5.cloned.1.call-update) | async-done | bytes 1966096 | tf_op jit(solution)/shard_map/all_gather | solution.py:16
  57.4 8.7 %fusion.9 = f32[1280,1536]{1,0:T(8,128)} fusion(bf16[1280,768]{1,0:T(8,128)(2,1)} %all-gather.5.cloned.1.call-done, bf16[1536,768]{1,0:T(8,128)(2,1)} %param.9), kind=kOutput, calls=%fused_computation.15 | convolution fusion | flops 3019898880 | bytes 12189696 | tf_op jit(solution)/shard_map/td,fd->tf/dot_general | solution.py:34
  66.1 37.5 %all-gather.3.cloned.1.call-done = bf16[1280,768]{1,0:T(8,128)(2,1)} async-done(((bf16[80,768]{1,0:T(8,128)(2,1)}), bf16[1280,768]{1,0:T(8,128)(2,1)}) %all-gather.3.cloned.1.call-update) | async-done | bytes 1966096 | tf_op jit(solution)/shard_map/all_gather | solution.py:15
  103.5 0.0 copy-done
  103.5 7.0 %fusion.7 = f32[1280,1536]{1,0:T(8,128)} fusion(bf16[1280,768]{1,0:T(8,128)(2,1)} %all-gather.3.cloned.1.call-done, bf16[768,1536]{1,0:T(8,128)(2,1)S(1)} %copy-done), kind=kOutput, calls=%fused_computation.13 | convolution fusion | flops 3019898880 | bytes 12189696 | tf_op jit(solution)/shard_map/dot_general | solution.py:18
  110.5 0.0 copy-start.4
  110.5 0.0 all-reduce.3.cloned.1.call-update
  110.5 0.0 reduce-scatter.5.cloned.1.call-start
  110.6 173.0 %all-reduce.3.cloned.1.call-done = (f32[1280,1536]{1,0:T(8,128)}, f32[1280,1536]{1,0:T(8,128)}) async-done(((f32[1280,1536]{1,0:T(8,128)}, f32[1280,1536]{1,0:T(8,128)}), (f32[1280,1536]{1,0:T(8,128)}, f32[1280,1536]{1,0:T(8,128)})) %all-reduce.3.cloned.1.call-update) | async-done | bytes 15728656 | tf_op jit(solution)/shard_map/psum | solution.py:19
  283.6 0.0 copy-done.4
  283.6 10.6 %convert_reduce_fusion = (f32[1536]{0:T(1024)}, bf16[1280,1536]{1,0:T(8,128)(2,1)S(1)}, bf16[1280,1536]{1,0:T(8,128)(2,1)}) fusion(f32[1280,1536]{1,0:T(8,128)} %get-tuple-element.13, f32[1280,1536]{1,0:T(8,128)} %get-tuple-element.12, f32[1536]{0:T(1024)S(1)} %copy-done.4), kind=kLoop, calls=%fused_computation.7 | loop fusion | flops 29489664 | bytes 23605248 | tf_op jit(solution)/shard_map/reduce_sum | solution.py:37
  294.2 0.0 copy-start.2
  294.2 1.9 copy-done.2
  296.1 5.1 %fusion.10 = f32[1280,768]{1,0:T(8,128)} fusion(bf16[1280,1536]{1,0:T(8,128)(2,1)S(1)} %get-tuple-element.15, bf16[768,1536]{1,0:T(8,128)(2,1)S(1)} %copy-done), kind=kOutput, calls=%fused_computation.16 | convolution fusion | flops 3019898880 | bytes 10223616 | tf_op jit(solution)/shard_map/tf,df->td/dot_general | solution.py:41
  301.2 0.0 copy-start.6
  301.2 0.0 reduce-scatter.5.cloned.1.call-update
  301.3 0.2 reduce-scatter.3.cloned.1.call-start
  301.5 1.4 copy-done.6
  302.9 7.2 %fusion.8 = f32[1280,768]{1,0:T(8,128)} fusion(bf16[1280,1536]{1,0:T(8,128)(2,1)} %get-tuple-element.16, bf16[1536,768]{1,0:T(8,128)(2,1)S(1)} %copy-done.6), kind=kOutput, calls=%fused_computation.14 | convolution fusion | flops 3019898880 | bytes 10223616 | tf_op jit(solution)/shard_map/dot_general | solution.py:25
  310.1 0.0 copy-start.3
  310.1 0.0 reduce-scatter.3.cloned.1.call-update
  310.1 1.6 copy-done.3
  311.7 0.9 convert_reduce_fusion.1
  312.6 8.2 %convolution_bitcast_fusion = f32[768,1536]{0,1:T(8,128)} fusion(bf16[1280,1536]{1,0:T(8,128)(2,1)} %copy-done.2, bf16[1280,768]{1,0:T(8,128)(2,1)} %all-gather.3.cloned.1.call-done), kind=kOutput, calls=%fused_computation.11 | convolution fusion | flops 3019898880 | bytes 10616832 | tf_op jit(solution)/shard_map/td,tf->df/dot_general | solution.py:38
  320.8 6.1 %copy.12 = f32[768,1536]{1,0:T(8,128)} copy(f32[768,1536]{0,1:T(8,128)} %convolution_bitcast_fusion) | data formatting | bytes 9437184
  327.0 0.0 copy-start.5
  327.0 0.0 copy-start.1
  327.0 8.4 %fusion.11 = f32[1536,768]{1,0:T(8,128)} fusion(bf16[1280,1536]{1,0:T(8,128)(2,1)} %get-tuple-element.16, bf16[1280,768]{1,0:T(8,128)(2,1)} %all-gather.5.cloned.1.call-done), kind=kOutput, calls=%fused_computation.17 | convolution fusion | flops 3019898880 | bytes 10616832 | tf_op jit(solution)/shard_map/tf,td->fd/dot_general | solution.py:33
  335.4 42.9 %reduce-scatter.5.cloned.1.call-done = f32[80,768]{1,0:T(8,128)} async-done(((f32[1280,768]{1,0:T(8,128)}), f32[80,768]{1,0:T(8,128)}) %reduce-scatter.5.cloned.1.call-update) | async-done | bytes 245776 | tf_op jit(solution)/shard_map/reduce_scatter | solution.py:40
  378.3 1.6 convert_element_type.21
  379.9 77.8 %reduce-scatter.3.cloned.1.call-done = f32[80,768]{1,0:T(8,128)} async-done(((f32[1280,768]{1,0:T(8,128)}), f32[80,768]{1,0:T(8,128)}) %reduce-scatter.3.cloned.1.call-update) | async-done | bytes 245776 | tf_op jit(solution)/shard_map/reduce_scatter | solution.py:24
  457.7 0.0 copy-done.5
  457.7 1.6 add_convert_fusion
  459.3 0.0 copy-done.1
Async XLA Ops:
  7.2 96.4 %copy-start = (bf16[768,1536]{1,0:T(8,128)(2,1)S(1)}, bf16[768,1536]{1,0:T(8,128)(2,1)}, u32[]{:S(2)}) copy-start(bf16[768,1536]{1,0:T(8,128)(2,1)} %param.7) | copy-start | bytes 7077892
  7.2 50.2 %all-gather.5.cloned.1.call-start = ((), (), s32[]{:S(2)}) async-start(), calls=%async_computation.4 | async-start | bytes 2088960 | tf_op jit(solution)/shard_map/all_gather | solution.py:16
  7.9 95.6 %all-gather.3.cloned.1.call-start = ((), (), s32[]{:S(2)}) async-start(), calls=%async_computation.2 | async-start | bytes 2088960 | tf_op jit(solution)/shard_map/all_gather | solution.py:15
  8.7 274.9 %all-reduce.3.cloned.1.call-start = ((), (), s32[]{:S(2)}) async-start(), calls=%async_computation.6 | async-start | bytes 31457280 | tf_op jit(solution)/shard_map/psum | solution.py:19
  110.5 173.1 %copy-start.4 = (f32[1536]{0:T(1024)S(1)}, f32[1536]{0:T(1024)}, u32[]{:S(2)}) copy-start(f32[1536]{0:T(1024)} %param.8) | copy-start | bytes 18436
  110.5 267.7 %reduce-scatter.5.cloned.1.call-start = ((), (), s32[]{:S(2)}) async-start(), calls=%async_computation.5 | async-start | bytes 4177920 | tf_op jit(solution)/shard_map/reduce_scatter | solution.py:40
  294.2 1.9 copy-start.2
  301.2 1.7 copy-start.6
  301.3 156.4 %reduce-scatter.3.cloned.1.call-start = ((), (), s32[]{:S(2)}) async-start(), calls=%async_computation.3 | async-start | bytes 4177920 | tf_op jit(solution)/shard_map/reduce_scatter | solution.py:24
  310.1 1.6 copy-start.3
  327.0 130.7 %copy-start.5 = (f32[768]{0:T(1024)S(1)}, f32[768]{0:T(1024)}, u32[]{:S(2)}) copy-start(f32[768]{0:T(1024)} %param.10) | copy-start | bytes 9220
  327.0 132.3 %copy-start.1 = (bf16[768,1536]{1,0:T(8,128)(2,1)S(1)}, bf16[768,1536]{1,0:T(8,128)(2,1)}, u32[]{:S(2)}) copy-start(bf16[768,1536]{1,0:T(8,128)(2,1)} %param.7) | copy-start | bytes 7077892
Sparse Core Ops, SparseCore 0:
  10.2 47.1 all-gather.4
  59.5 43.9 all-gather.2
  110.6 172.8 all-reduce.2
  301.4 76.8 reduce-scatter.4
  381.5 76.1 reduce-scatter.2
where the time goes:
time: 466 us
  waiting for transfers between devices  381 us (82%)
  matrix products  44.6 us (10%)
  other arithmetic  14.7 us (3%)
  between operations  13.8 us (3%)
  local copies, waits for them, and re-layouts  11 us (2%)
    psum x1, waiting for transfers between devices, shards(): hidden = lax.psum(partial_value, 'row') + b_in  173 us
    reduce_scatter x1, waiting for transfers between devices, shards(): lax.psum_scatter(jnp.dot(rows, w_out, preferred_element_type=jnp.float32)...  77.8 us
    all_gather x1, waiting for transfers between devices, shards(): lax.all_gather(out_grad, 'col', axis=0, tiled=True)  48.7 us
    reduce_scatter x1, waiting for transfers between devices, shards(): lax.psum_scatter(jnp.einsum('tf,df->td', rows, w_in, preferred_element_ty...  42.9 us
    all_gather x1, waiting for transfers between devices, shards(): lax.all_gather(inputs, 'col', axis=0, tiled=True)  37.5 us
    unnamed x15, local copies, waits for them, and re-layouts  11 us
    reduce_sum x1, other arithmetic, shards(): b_in_grad = jnp.sum(pre_grad, axis=0, dtype=jnp.float32)  10.6 us
  transfers between devices with their start and end apart: 5, of which 5 were waited for; matrix products, arithmetic and copies ran while one was open for 9% of the time, Pallas kernels for 0%

commit v1 on v0

v1 whole, which is shorter than its diff:
```python
import jax
import jax.numpy as jnp
from jax import lax
from jax.experimental import pallas as pl
from jax.experimental.pallas import tpu as pltpu
from jax.sharding import PartitionSpec as P

MESH = pl.DeviceIdType.MESH
BF16 = jnp.bfloat16
F32 = jnp.float32

CH = 5
TB = 16
ROWS = 256
HALF = ROWS // 2
DL = 768
FL = 1536
DH = DL // 2


def dot(a, b, dims):
    return lax.dot_general(a, b, ((dims[:1], dims[1:]), ((), ())), preferred_element_type=F32)


def body(
    x_hbm, g_hbm, w_in_hbm, w_out_hbm, b_in, b_out,
    out_o, out_i, out_w1, out_b1, out_w2, out_b2,
    xg, w_in, w_out, snd, crv, own, s, r1b, r2b, act, part, ra, rb, sa, sb, ta, tb, w1g, w2g, b1g, b2g,
    load_sem, ag1_s, ag1_r, ag2_s, ag2_r, ce_s, ce_r, y_s, y_r, gc_s, gc_r, rs1_s, rs1_r, rs2_s, rs2_r, st_sem,
):
    row, col = lax.axis_index("row"), lax.axis_index("col")
    y, core = row // 2, row % 2
    z, x = col // 4, col % 4
    abit, bbit = ((y + 1) // 2) % 2, y // 2
    ya, yb = y + 1 - 2 * (y % 2), 3 - y
    pair_a, pair_b = (ya * 2 + core, col), (yb * 2 + core, col)
    mate = (y * 2 + 1 - core, col)

    def zx(dz, dx):
        return (row, ((z + dz) % 4) * 4 + (x + dx) % 4)

    loads = [
        pltpu.make_async_copy(x_hbm, xg.at[:, 0, z, x], load_sem.at[0]),
        pltpu.make_async_copy(g_hbm, xg.at[:, 1, z, x], load_sem.at[1]),
        pltpu.make_async_copy(w_in_hbm, w_in, load_sem.at[2]),
        pltpu.make_async_copy(w_out_hbm, w_out, load_sem.at[3]),
    ]
    for cp in loads:
        cp.start()

    barrier = pltpu.get_barrier_semaphore()
    peers = [pair_a, pair_b, mate] + [zx(0, d) for d in (1, 2, 3)] + [zx(d, 0) for d in (1, 2, 3)]
    for p in peers:
        pl.semaphore_signal(barrier, inc=1, device_id=p, device_id_type=MESH)
    pl.semaphore_wait(barrier, len(peers))
    loads[0].wait()
    loads[1].wait()

    def rcopy(src, dst, ss, rs, dev):
        return pltpu.make_async_remote_copy(
            src_ref=src, dst_ref=dst, send_sem=ss, recv_sem=rs, device_id=dev, device_id_type=MESH
        )

    lo, hi = pl.ds(0, DH), pl.ds(DH, DH)

    def ag1(c):
        res = []
        for d in (1, 2, 3):
            ref = xg.at[c, :, z, x, :, lo]
            res.append(rcopy(ref, ref, ag1_s.at[c, d - 1], ag1_r.at[c, d - 1], zx(0, d)))
            ref = xg.at[c, :, z, x, :, hi]
            res.append(rcopy(ref, ref, ag1_s.at[c, d + 2], ag1_r.at[c, d + 2], zx(d, 0)))
        return res

    def ag2(c):
        res = []
        for d in (1, 2, 3):
            ref = xg.at[c, :, z, :, :, lo]
            res.append(rcopy(ref, ref, ag2_s.at[c, d - 1], ag2_r.at[c, d - 1], zx(d, 0)))
            ref = xg.at[c, :, :, x, :, hi]
            res.append(rcopy(ref, ref, ag2_s.at[c, d + 2], ag2_r.at[c, d + 2], zx(0, d)))
        return res

    def core_swap(c):
        return [rcopy(snd, crv.at[c], ce_s.at[c], ce_r.at[c], mate)]

    def rows(start, n):
        return pl.ds(pl.multiple_of(start, TB), n)

    a_keep, a_send = abit * 32, (1 - abit) * 32
    b_keep, b_send = 64 + bbit * 32, 64 + (1 - bbit) * 32
    a_own, a_send2 = a_keep + bbit * 16, a_keep + (1 - bbit) * 16
    b_own, b_send2 = b_keep + abit * 16, b_keep + (1 - abit) * 16

    def y_red1(c):
        return [
            rcopy(s.at[c, :, rows(a_send, 32)], r1b.at[c, 0], y_s.at[c, 0], y_r.at[c, 0], pair_a),
            rcopy(s.at[c, :, rows(b_send, 32)], r1b.at[c, 1], y_s.at[c, 1], y_r.at[c, 1], pair_b),
        ]

    def y_red2(c):
        return [
            rcopy(s.at[c, :, rows(a_send2, 16)], r2b.at[c, 0], y_s.at[c, 2], y_r.at[c, 2], pair_b),
            rcopy(s.at[c, :, rows(b_send2, 16)], r2b.at[c, 1], y_s.at[c, 3], y_r.at[c, 3], pair_a),
        ]

    def y_gat1(c):
        ref_a = act.at[c, :, rows(core * HALF + a_own, 16)]
        ref_b = act.at[c, :, rows(core * HALF + b_own, 16)]
        return [
            rcopy(ref_a, ref_a, y_s.at[c, 4], y_r.at[c, 4], pair_b),
            rcopy(ref_b, ref_b, y_s.at[c, 5], y_r.at[c, 5], pair_a),
        ]

    def y_gat2(c):
        ref_a = act.at[c, :, rows(core * HALF + a_keep, 32)]
        ref_b = act.at[c, :, rows(core * HALF + b_keep, 32)]
        return [
            rcopy(ref_a, ref_a, y_s.at[c, 6], y_r.at[c, 6], pair_a),
            rcopy(ref_b, ref_b, y_s.at[c, 7], y_r.at[c, 7], pair_b),
        ]

    def core_gat(c):
        ref = act.at[c, :, rows(core * HALF, HALF)]
        return [rcopy(ref, ref, gc_s.at[c], gc_r.at[c], mate)]

    def rs1(c):
        res = []
        for d in (1, 2, 3):
            src = part.at[c, :, :, (x + d) % 4, :, lo]
            res.append(rcopy(src, ra.at[c, d - 1], rs1_s.at[c, d - 1], rs1_r.at[c, d - 1], zx(0, d)))
            src = part.at[c, :, (z + d) % 4, :, :, hi]
            res.append(rcopy(src, rb.at[c, d - 1], rs1_s.at[c, d + 2], rs1_r.at[c, d + 2], zx(d, 0)))
        return res

    def rs2(c):
        res = []
        for d in (1, 2, 3):
            src = sa.at[c, :, (z + d) % 4]
            res.append(rcopy(src, ta.at[c, d - 1], rs2_s.at[c, d - 1], rs2_r.at[c, d - 1], zx(d, 0)))
            src = sb.at[c, :, (x + d) % 4]
            res.append(rcopy(src, tb.at[c, d - 1], rs2_s.at[c, d + 2], rs2_r.at[c, d + 2], zx(0, d)))
        return res

    def start(copies):
        for cp in copies:
            cp.start()

    def wait(copies):
        for cp in copies:
            cp.wait()

    w1g[...] = jnp.zeros_like(w1g)
    w2g[...] = jnp.zeros_like(w2g)
    b1g[...] = jnp.zeros_like(b1g)
    b2g[...] = jnp.zeros_like(b2g)

    def half_of(c, t, which):
        return xg[c, t, pl.ds(2 * which, 2)].reshape(HALF, DL)

    def chunk_of(c, t):
        return xg[c, t].reshape(ROWS, DL)

    @pl.loop(0, CH + 9)
    def _(i):
        def stage(offset, fn):
            c = i - offset
            pl.when(jnp.logical_and(c >= 0, c < CH))(lambda: fn(c))

        def red2_stage(c):
            wait(y_red1(c))
            for k, keep in ((0, a_keep), (1, b_keep)):
                here = s.at[c, :, rows(keep, 32)]
                here[...] = (here[...].astype(F32) + r1b[c, k].astype(F32)).astype(BF16)
            start(y_red2(c))

        def gelu_stage(c):
            wait(y_red2(c))
            for k, mine in ((0, a_own), (1, b_own)):
                total = s[c, :, rows(mine, 16)].astype(F32) + r2b[c, k].astype(F32)
                hidden = total[0] + b_in[...]
                half = 0.5 * (1.0 + lax.erf(hidden * 0.7071067811865476))
                slope = half + hidden * jnp.exp(-0.5 * hidden * hidden) * 0.3989422804014327
                at = rows(core * HALF + mine, 16)
                act[c, 0, at] = (hidden * half).astype(BF16)
                act[c, 1, at] = (total[1] * slope).astype(BF16)
            start(y_gat1(c))

        def gat2_stage(c):
            wait(y_gat1(c))
            start(y_gat2(c))

        def core_gat_stage(c):
            wait(y_gat2(c))
            start(core_gat(c))

        def ag1_stage(c):
            start(ag1(c))

        def ag2_stage(c):
            wait(ag1(c))
            start(ag2(c))

        def hidden_stage(c):
            @pl.when(c == 0)
            def _():
                loads[2].wait()
                loads[3].wait()

            wait(ag2(c))
            lhs = jnp.concatenate([half_of(c, 0, 1 - core), half_of(c, 0, core)], axis=0)
            for n in range(0, FL, 512):
                r = dot(lhs, w_in[:, n:n + 512], (1, 0))
                snd[0, :, n:n + 512] = r[:HALF].astype(BF16)
                own[0, :, n:n + 512] = r[HALF:]
            lhs = jnp.concatenate([half_of(c, 1, 1 - core), half_of(c, 1, core)], axis=0)
            for n in range(0, FL, 512):
                r = dot(lhs, w_out[n:n + 512, :], (1, 1))
                snd[1, :, n:n + 512] = r[:HALF].astype(BF16)
                own[1, :, n:n + 512] = r[HALF:]
            start(core_swap(c))

        def out_stage(c):
            wait(core_gat(c))
            for n in range(0, DL, 256):
                r = dot(act[c, 0], w_out[:, n:n + 256], (1, 0))
                part[c, 0, :, :, :, n:n + 256] = r.astype(BF16).reshape(4, 4, TB, 256)
            for n in range(0, DL, 256):
                r = dot(act[c, 1], w_in[n:n + 256, :], (1, 1))
                part[c, 1, :, :, :, n:n + 256] = r.astype(BF16).reshape(4, 4, TB, 256)
            start(rs1(c))

        def red1_stage(c):
            wait(core_swap(c))
            s[c] = (own[...] + crv[c].astype(F32)).astype(BF16)
            start(y_red1(c))

        def rs2_stage(c):
            wait(rs1(c))
            total = part[c, :, :, x, :, lo].astype(F32)
            for d in range(3):
                total += ra[c, d].astype(F32)
            sa[c] = total.astype(BF16)
            total = part[c, :, z, :, :, hi].astype(F32)
            for d in range(3):
                total += rb[c, d].astype(F32)
            sb[c] = total.astype(BF16)
            start(rs2(c))

        def final_stage(c):
            wait(rs2(c))
            for buf, got, me, cols in ((sa, ta, z, lo), (sb, tb, x, hi)):
                total = buf[c, :, me].astype(F32)
                for d in range(3):
                    total += got[c, d].astype(F32)
                out_o[c, :, cols] = (total[0] + b_out[:, cols]).astype(BF16)
                out_i[c, :, cols] = total[1].astype(BF16)

        def weight_stage(c):
            g_k = chunk_of(c, 1)
            for n in range(0, FL, 512):
                w2g[n:n + 512, :] += dot(act[c, 0, :, n:n + 512], g_k, (0, 0))
            x_k = chunk_of(c, 0)
            for n in range(0, FL, 512):
                w1g[:, n:n + 512] += dot(x_k, act[c, 1, :, n:n + 512], (0, 0))
            b1g[...] += jnp.sum(act[c, 1].astype(F32), axis=0, keepdims=True)
            b2g[...] += jnp.sum(g_k.astype(F32), axis=0, keepdims=True)

        stage(3, red2_stage)
        stage(4, gelu_stage)
        stage(5, gat2_stage)
        stage(6, core_gat_stage)
        stage(1, ag2_stage)
        stage(0, ag1_stage)
        stage(2, hidden_stage)
        stage(6, out_stage)
        stage(2, red1_stage)
        stage(7, rs2_stage)
        stage(8, final_stage)
        stage(6, weight_stage)

    stores = [
        pltpu.make_async_copy(w1g, out_w1, st_sem.at[0]),
        pltpu.make_async_copy(w2g, out_w2, st_sem.at[1]),
    ]
    for cp in stores:
        cp.start()
    out_b1[...] = b1g[...]
    out_b2[...] = b2g[...]
    for cp in stores:
        cp.wait()


def shards(inputs, w_in, b_in, w_out, b_out, out_grad):
    any_spec = pl.BlockSpec(memory_space=pl.ANY)
    vmem_spec = pl.BlockSpec(memory_space=pltpu.VMEM)
    dma = pltpu.SemaphoreType.DMA
    outs = pl.pallas_call(
        body,
        out_shape=[
            jax.ShapeDtypeStruct((CH, TB, DL), BF16),
            jax.ShapeDtypeStruct((CH, TB, DL), BF16),
            jax.ShapeDtypeStruct((DL, FL), F32),
            jax.ShapeDtypeStruct((1, FL), F32),
            jax.ShapeDtypeStruct((FL, DL), F32),
            jax.ShapeDtypeStruct((1, DL), F32),
        ],
        in_specs=[any_spec] * 4 + [vmem_spec] * 2,
        out_specs=[vmem_spec, vmem_spec, any_spec, vmem_spec, any_spec, vmem_spec],
        scratch_shapes=[
            pltpu.VMEM((CH, 2, 4, 4, TB, DL), BF16),
            pltpu.VMEM((DL, FL), BF16),
            pltpu.VMEM((FL, DL), BF16),
            pltpu.VMEM((2, HALF, FL), BF16),
            pltpu.VMEM((CH, 2, HALF, FL), BF16),
            pltpu.VMEM((2, HALF, FL), F32),
            pltpu.VMEM((CH, 2, HALF, FL), BF16),
            pltpu.VMEM((CH, 2, 2, 32, FL), BF16),
            pltpu.VMEM((CH, 2, 2, 16, FL), BF16),
            pltpu.VMEM((CH, 2, ROWS, FL), BF16),
            pltpu.VMEM((CH, 2, 4, 4, TB, DL), BF16),
            pltpu.VMEM((CH, 3, 2, 4, TB, DH), BF16),
            pltpu.VMEM((CH, 3, 2, 4, TB, DH), BF16),
            pltpu.VMEM((CH, 2, 4, TB, DH), BF16),
            pltpu.VMEM((CH, 2, 4, TB, DH), BF16),
            pltpu.VMEM((CH, 3, 2, TB, DH), BF16),
            pltpu.VMEM((CH, 3, 2, TB, DH), BF16),
            pltpu.VMEM((DL, FL), F32),
            pltpu.VMEM((FL, DL), F32),
            pltpu.VMEM((1, FL), F32),
            pltpu.VMEM((1, DL), F32),
            dma((4,)),
            dma((CH, 6)), dma((CH, 6)), dma((CH, 6)), dma((CH, 6)),
            dma((CH,)), dma((CH,)),
            dma((CH, 8)), dma((CH, 8)),
            dma((CH,)), dma((CH,)),
            dma((CH, 6)), dma((CH, 6)), dma((CH, 6)), dma((CH, 6)),
            dma((2,)),
        ],
        compiler_params=pltpu.CompilerParams(
            collective_id=0, has_side_effects=True, vmem_limit_bytes=60 * 2**20
        ),
        cost_estimate=pl.CostEstimate(flops=18 * 10**9, bytes_accessed=15 * 10**6, transcendentals=10**6),
        name="mlp",
    )(
        inputs.reshape(CH, TB, DL), out_grad.reshape(CH, TB, DL), w_in, w_out,
        b_in.reshape(1, FL), b_out.reshape(1, DL),
    )
    output, input_grad, w_in_grad, b_in_grad, w_out_grad, b_out_grad = outs
    return (
        output.reshape(CH * TB, DL), input_grad.reshape(CH * TB, DL),
        w_in_grad, b_in_grad.reshape(FL), w_out_grad, b_out_grad.reshape(DL),
    )


def solution(mesh):
    placed = (
        P("col", "row"),
        P("row", "col"),
        P("col"),
        P("col", "row"),
        P("row"),
        P("col", "row"),
    )
    return jax.shard_map(
        shards,
        mesh=mesh,
        in_specs=placed,
        out_specs=(
            P("col", "row"),
            P("col", "row"),
            P("row", "col"),
            P("col"),
            P("col", "row"),
            P("row"),
        ),
        check_vma=False,
    )
```

time: 466 us -> 143 us (0.31)
  waiting for transfers between devices: 381 us -> 0 us
  Pallas kernels: 0 us -> 127 us
  matrix products: 44.6 us -> 0 us
  between operations: 13.8 us -> 0.65 us
  other arithmetic: 14.7 us -> 2.6 us
    psum x1 -> x0, waiting for transfers between devices: 173 us -> none  [shards(): hidden = lax.psum(partial_value, 'row') + b_in]
    pallas_call x0 -> x1, Pallas kernels: none -> 127 us  [shards(): pl.pallas_call(body, out_shape=[jax.ShapeDtypeStruct((CH, TB, DL), BF16),...]
    reduce_scatter x2 -> x0, waiting for transfers between devices: 121 us -> none  [the longest x1 77.8 us: shards(): lax.psum_scatter(jnp.dot(rows, w_out, preferred_element_type=jnp.float32)...]
    all_gather x2 -> x0, waiting for transfers between devices: 86.1 us -> none  [the longest x1 48.7 us: shards(): lax.all_gather(out_grad, 'col', axis=0, tiled=True)]
    dot_general x6 -> x0, matrix products: 44.6 us -> none  [the longest x1 8.68 us: shards(): jnp.einsum('td,fd->tf', grad_all, w_out, preferred_element_type=jnp.float32)]
    reduce_sum x2 -> x0, other arithmetic: 11.5 us -> none  [the longest x1 10.6 us: shards(): b_in_grad = jnp.sum(pre_grad, axis=0, dtype=jnp.float32)]
    unnamed x15 -> x8, local copies, waits for them, and re-layouts: 11 us -> 10.4 us
  transfers between devices with their start and end apart: 5 -> 0, of which waited for: 5 -> 0; matrix products, arithmetic and copies ran while one was open for 9% -> 0% of each run, Pallas kernels for 0% -> 0%
where the time goes in v1:
time: 143 us
  Pallas kernels  127 us (89%)
  local copies, waits for them, and re-layouts  12.9 us (9%)
  other arithmetic  2.6 us (2%)
    pallas_call x1, Pallas kernels, shards(): pl.pallas_call(body, out_shape=[jax.ShapeDtypeStruct((CH, TB, DL), BF16),...  127 us
    unnamed x8, local copies, waits for them, and re-layouts  10.4 us

profile of v1, /device:TPU:0, one launch (start us, length us, event | category | flops | bytes accessed | tf_op | source)
XLA Modules:
  0.0 143.0 jit_solution(3492268005086081219)
XLA Ops:
  0.6 1.3 reshape.38.b_in
  1.9 1.3 reshape.39.b_out
  3.2 126.8 %mlp.1 = (bf16[5,16,768]{2,1,0:T(8,128)(2,1)}, bf16[5,16,768]{2,1,0:T(8,128)(2,1)}, f32[768,1536]{1,0:T(8,128)}, f32[1,1536]{1,0:T(1,128)}, f32[1536,768]{1,0:T(8,128)}, /*index=5*/f32[1,768]{1,0:T(1,128)}) custom-call(bf16[5,16,768]{2,1,0:T(8,128)(2,1)} %bitcast.8, bf16[5,16,768]{2,1,0:T(8,128)(2,1)} %bitcast.9, bf16[768,1536]{1,0:T(8,128)(2,1)} %w_in_hbm.1, ...), custom_call_target="tpu_custom_call" | custom-call | flops 17999998976 | bytes 15000000 | tf_op jit(solution)/shard_map/mlp/pallas_call | solution.py:298
  130.0 1.3 reduce
  131.3 1.3 reduce.1
  132.6 1.6 %copy.16 = bf16[80,768]{1,0:T(8,128)(2,1)} copy(bf16[80,768]{1,0:T(8,128)(2,1)} %bitcast.7) | data formatting | bytes 245760
  134.2 0.0 slice-start
  134.2 1.7 %copy.17 = bf16[80,768]{1,0:T(8,128)(2,1)} copy(bf16[80,768]{1,0:T(8,128)(2,1)} %bitcast.6) | data formatting | bytes 245760
  135.9 0.0 slice-start.1
  135.9 4.9 %copy.18 = f32[768,1536]{1,0:T(8,128)} copy(f32[768,1536]{1,0:T(8,128)} %get-tuple-element.26) | data formatting | bytes 9437184
  140.8 0.0 slice-done
  140.8 0.0 slice-done.1
  140.8 2.2 %copy.19 = f32[1536,768]{1,0:T(8,128)} copy(f32[1536,768]{1,0:T(8,128)S(1)} %bitcast.5) | data formatting | bytes 9437184
  (1 shorter events, 0.0 us)
Async XLA Ops:
  134.2 6.6 %slice-start = ((s8[4718592]{0:T(1024)(128)(4,1)}), s8[4194304]{0:T(1024)(128)(4,1)S(1)}, s32[]{:S(2)}) async-start(s8[4718592]{0:T(1024)(128)(4,1)} %bitcast.4), calls=%async_computation | async-start | bytes 8388608
  135.9 4.9 %slice-start.1 = ((s8[4718592]{0:T(1024)(128)(4,1)}), s8[524288]{0:T(1024)(128)(4,1)S(1)}, s32[]{:S(2)}) async-start(s8[4718592]{0:T(1024)(128)(4,1)} %bitcast.4), calls=%async_computation.1 | async-start | bytes 1048576

commit v2 on v1

--- a/solution.py
+++ b/solution.py
@@ -24,9 +24,9 @@
 
 def body(
     x_hbm, g_hbm, w_in_hbm, w_out_hbm, b_in, b_out,
-    out_o, out_i, out_w1, out_b1, out_w2, out_b2,
-    xg, w_in, w_out, snd, crv, own, s, r1b, r2b, act, part, ra, rb, sa, sb, ta, tb, w1g, w2g, b1g, b2g,
-    load_sem, ag1_s, ag1_r, ag2_s, ag2_r, ce_s, ce_r, y_s, y_r, gc_s, gc_r, rs1_s, rs1_r, rs2_s, rs2_r, st_sem,
+    out_o, out_i, w1g, out_b1, w2g, out_b2,
+    xg, w_in, w_out, snd, crv, own, s, r1b, r2b, act, part, ra, rb, sa, sb, ta, tb, b1g, b2g,
+    load_sem, ag1_s, ag1_r, ag2_s, ag2_r, ce_s, ce_r, y_s, y_r, gc_s, gc_r, rs1_s, rs1_r, rs2_s, rs2_r,
 ):
     row, col = lax.axis_index("row"), lax.axis_index("col")
     y, core = row // 2, row % 2
@@ -178,7 +178,7 @@
             wait(y_red2(c))
             for k, mine in ((0, a_own), (1, b_own)):
                 total = s[c, :, rows(mine, 16)].astype(F32) + r2b[c, k].astype(F32)
-                hidden = total[0] + b_in[...]
+                hidden = total[0] + b_in[...][None]
                 half = 0.5 * (1.0 + lax.erf(hidden * 0.7071067811865476))
                 slope = half + hidden * jnp.exp(-0.5 * hidden * hidden) * 0.3989422804014327
                 at = rows(core * HALF + mine, 16)
@@ -253,7 +253,7 @@
                 total = buf[c, :, me].astype(F32)
                 for d in range(3):
                     total += got[c, d].astype(F32)
-                out_o[c, :, cols] = (total[0] + b_out[:, cols]).astype(BF16)
+                out_o[c, :, cols] = (total[0] + b_out[cols][None]).astype(BF16)
                 out_i[c, :, cols] = total[1].astype(BF16)
 
         def weight_stage(c):
@@ -266,28 +266,29 @@
             b1g[...] += jnp.sum(act[c, 1].astype(F32), axis=0, keepdims=True)
             b2g[...] += jnp.sum(g_k.astype(F32), axis=0, keepdims=True)
 
-        stage(3, red2_stage)
-        stage(4, gelu_stage)
-        stage(5, gat2_stage)
-        stage(6, core_gat_stage)
+        stage(6, gat2_stage)
+        stage(5, gelu_stage)
+        stage(4, red2_stage)
+        stage(3, red1_stage)
+        stage(7, core_gat_stage)
         stage(1, ag2_stage)
         stage(0, ag1_stage)
         stage(2, hidden_stage)
-        stage(6, out_stage)
-        stage(2, red1_stage)
-        stage(7, rs2_stage)
-        stage(8, final_stage)
-        stage(6, weight_stage)
-
-    stores = [
-        pltpu.make_async_copy(w1g, out_w1, st_sem.at[0]),
-        pltpu.make_async_copy(w2g, out_w2, st_sem.at[1]),
-    ]
-    for cp in stores:
+        stage(9, final_stage)
+        stage(8, rs2_stage)
+        stage(7, out_stage)
+        stage(7, weight_stage)
+
+    out_b1[...] = jnp.sum(b1g[...], axis=0)
+    out_b2[...] = jnp.sum(b2g[...], axis=0)
+
+
+def write_out(*refs):
+    sems = refs[-1]
+    copies = [pltpu.make_async_copy(refs[k], refs[k + 6], sems.at[k]) for k in range(6)]
+    for cp in copies:
         cp.start()
-    out_b1[...] = b1g[...]
-    out_b2[...] = b2g[...]
-    for cp in stores:
+    for cp in copies:
         cp.wait()
 
 
@@ -298,15 +299,15 @@
     outs = pl.pallas_call(
         body,
         out_shape=[
-            jax.ShapeDtypeStruct((CH, TB, DL), BF16),
-            jax.ShapeDtypeStruct((CH, TB, DL), BF16),
-            jax.ShapeDtypeStruct((DL, FL), F32),
-            jax.ShapeDtypeStruct((1, FL), F32),
-            jax.ShapeDtypeStruct((FL, DL), F32),
-            jax.ShapeDtypeStruct((1, DL), F32),
+            pltpu.VMEM((CH, TB, DL), BF16),
+            pltpu.VMEM((CH, TB, DL), BF16),
+            pltpu.VMEM((DL, FL), F32),
+            pltpu.VMEM((FL,), F32),
+            pltpu.VMEM((FL, DL), F32),
+            pltpu.VMEM((DL,), F32),
         ],
         in_specs=[any_spec] * 4 + [vmem_spec] * 2,
-        out_specs=[vmem_spec, vmem_spec, any_spec, vmem_spec, any_spec, vmem_spec],
+        out_specs=[vmem_spec] * 6,
         scratch_shapes=[
             pltpu.VMEM((CH, 2, 4, 4, TB, DL), BF16),
             pltpu.VMEM((DL, FL), BF16),
@@ -325,8 +326,6 @@
             pltpu.VMEM((CH, 2, 4, TB, DH), BF16),
             pltpu.VMEM((CH, 3, 2, TB, DH), BF16),
             pltpu.VMEM((CH, 3, 2, TB, DH), BF16),
-            pltpu.VMEM((DL, FL), F32),
-            pltpu.VMEM((FL, DL), F32),
             pltpu.VMEM((1, FL), F32),
             pltpu.VMEM((1, DL), F32),
             dma((4,)),
@@ -335,22 +334,27 @@
             dma((CH, 8)), dma((CH, 8)),
             dma((CH,)), dma((CH,)),
             dma((CH, 6)), dma((CH, 6)), dma((CH, 6)), dma((CH, 6)),
-            dma((2,)),
         ],
         compiler_params=pltpu.CompilerParams(
-            collective_id=0, has_side_effects=True, vmem_limit_bytes=60 * 2**20
+            collective_id=0, has_side_effects=True, vmem_limit_bytes=48 * 2**20
         ),
         cost_estimate=pl.CostEstimate(flops=18 * 10**9, bytes_accessed=15 * 10**6, transcendentals=10**6),
         name="mlp",
     )(
         inputs.reshape(CH, TB, DL), out_grad.reshape(CH, TB, DL), w_in, w_out,
-        b_in.reshape(1, FL), b_out.reshape(1, DL),
+        b_in, b_out,
     )
-    output, input_grad, w_in_grad, b_in_grad, w_out_grad, b_out_grad = outs
-    return (
-        output.reshape(CH * TB, DL), input_grad.reshape(CH * TB, DL),
-        w_in_grad, b_in_grad.reshape(FL), w_out_grad, b_out_grad.reshape(DL),
-    )
+    outs = pl.pallas_call(
+        write_out,
+        out_shape=[jax.ShapeDtypeStruct(o.shape, o.dtype) for o in outs],
+        in_specs=[vmem_spec] * 6,
+        out_specs=[any_spec] * 6,
+        scratch_shapes=[dma((6,))],
+        compiler_params=pltpu.CompilerParams(vmem_limit_bytes=2**20),
+        name="write_out",
+    )(*[pltpu.with_memory_space_constraint(o, pltpu.VMEM) for o in outs])
+    output, input_grad, *grads = outs
+    return output.reshape(CH * TB, DL), input_grad.reshape(CH * TB, DL), *grads
 
 
 def solution(mesh):

time: 143 us -> 121 us (0.85)
  local copies, waits for them, and re-layouts: 12.9 us -> 0 us
  Pallas kernels: 127 us -> 120 us
  other arithmetic: 2.6 us -> 0 us
    unnamed x8 -> x0, local copies, waits for them, and re-layouts: 10.4 us -> none
    pallas_call x1 -> x2, Pallas kernels: 127 us -> 120 us  [the longest x1 116 us: shards(): pl.pallas_call(body, out_shape=[pltpu.VMEM((CH, TB, DL), BF16), pltpu.VME...]
    pallas_call x2 -> x0, other arithmetic: 2.6 us -> none  [shards(): pl.pallas_call(body, out_shape=[jax.ShapeDtypeStruct((CH, TB, DL), BF16),...]
    reshape x2 -> x0, local copies, waits for them, and re-layouts: 2.56 us -> none  [the longest x1 1.3 us: shards(): b_in.reshape(1, FL)]
where the time goes in v2:
time: 121 us
  Pallas kernels  120 us (99%)
    pallas_call x1, Pallas kernels, shards(): pl.pallas_call(body, out_shape=[pltpu.VMEM((CH, TB, DL), BF16), pltpu.VME...  116 us
    pallas_call x1, Pallas kernels, shards(): pl.pallas_call(write_out, out_shape=[jax.ShapeDtypeStruct(o.shape, o.dtyp...  3.88 us

profile of v2, /device:TPU:0, one launch (start us, length us, event | category | flops | bytes accessed | tf_op | source)
XLA Modules:
  0.0 120.7 jit_solution(6746016287925706288)
XLA Ops:
  0.6 116.2 %mlp.1 = (bf16[5,16,768]{2,1,0:T(8,128)(2,1)S(1)}, bf16[5,16,768]{2,1,0:T(8,128)(2,1)S(1)}, f32[768,1536]{1,0:T(8,128)S(1)}, f32[1536]{0:T(1024)S(1)}, f32[1536,768]{1,0:T(8,128)S(1)}, /*index=5*/f32[768]{0:T(1024)S(1)}) custom-call(bf16[5,16,768]{2,1,0:T(8,128)(2,1)} %bitcast.4, bf16[5,16,768]{2,1,0:T(8,128)(2,1)} %bitcast.5, bf16[768,1536]{1,0:T(8,128)(2,1)} %w_in_hbm.1, ...), custom_call_target="tpu_custom_call" | custom-call | flops 17999998976 | bytes 15000000 | tf_op jit(solution)/shard_map/mlp/pallas_call | solution.py:299
  116.8 3.9 %write_out.1 = (bf16[5,16,768]{2,1,0:T(8,128)(2,1)}, bf16[5,16,768]{2,1,0:T(8,128)(2,1)}, f32[768,1536]{1,0:T(8,128)}, f32[1536]{0:T(1024)}, f32[1536,768]{1,0:T(8,128)}, /*index=5*/f32[768]{0:T(1024)}) custom-call(bf16[5,16,768]{2,1,0:T(8,128)(2,1)S(1)} %get-tuple-element.18.refs_0_, bf16[5,16,768]{2,1,0:T(8,128)(2,1)S(1)} %get-tuple-element.19.refs_1_, ...), custom_call_target="tpu_custom_call" | custom-call | tf_op jit(solution)/shard_map/write_out/pallas_call | solution.py:347

commit v3 on v2

v3 whole, which is shorter than its diff:
```python
import jax
import jax.numpy as jnp
from jax import lax
from jax.experimental import pallas as pl
from jax.experimental.pallas import tpu as pltpu
from jax.sharding import PartitionSpec as P

MESH = pl.DeviceIdType.MESH
BF16 = jnp.bfloat16
F32 = jnp.float32

CH = 5
TB = 16
ROWS = 256
HALF = ROWS // 2
DL = 768
FL = 1536
DH = DL // 2


def dot(a, b, dims):
    return lax.dot_general(a, b, ((dims[:1], dims[1:]), ((), ())), preferred_element_type=F32)


def body(
    x_hbm, g_hbm, w_in_hbm, w_out_hbm, b_in_hbm, b_out_hbm,
    out_o, out_i, w1g, out_b1, w2g, out_b2,
    xg, w_in, w_out, snd, crv, own, s, r1b, r2b, act, part, rab, sab, tab, b1g, b2g, b_in, b_out,
    load_sem, ag1_s, ag1_r, ag2_s, ag2_r, ce_s, ce_r, y_s, y_r, gc_s, gc_r, rs1_s, rs1_r, rs2_s, rs2_r,
):
    row, col = lax.axis_index("row"), lax.axis_index("col")
    y, core = row // 2, row % 2
    z, x = col // 4, col % 4
    abit, bbit = ((y + 1) // 2) % 2, y // 2
    ya, yb = y + 1 - 2 * (y % 2), 3 - y
    pair_a, pair_b = (ya * 2 + core, col), (yb * 2 + core, col)
    mate = (y * 2 + 1 - core, col)

    def zx(dz, dx):
        return (row, ((z + dz) % 4) * 4 + (x + dx) % 4)

    loads = [
        pltpu.make_async_copy(x_hbm, xg.at[:, 0, z, x], load_sem.at[0]),
        pltpu.make_async_copy(g_hbm, xg.at[:, 1, z, x], load_sem.at[1]),
        pltpu.make_async_copy(w_in_hbm, w_in, load_sem.at[2]),
        pltpu.make_async_copy(w_out_hbm, w_out, load_sem.at[3]),
        pltpu.make_async_copy(b_in_hbm, b_in, load_sem.at[4]),
        pltpu.make_async_copy(b_out_hbm, b_out, load_sem.at[5]),
    ]
    for cp in loads:
        cp.start()

    barrier = pltpu.get_barrier_semaphore()
    peers = [pair_a, pair_b, mate] + [zx(0, d) for d in (1, 2, 3)] + [zx(d, 0) for d in (1, 2, 3)]
    for p in peers:
        pl.semaphore_signal(barrier, inc=1, device_id=p, device_id_type=MESH)
    pl.semaphore_wait(barrier, len(peers))
    loads[0].wait()
    loads[1].wait()

    def rcopy(src, dst, ss, rs, dev):
        return lambda: pltpu.make_async_remote_copy(
            src_ref=src, dst_ref=dst, send_sem=ss, recv_sem=rs, device_id=dev, device_id_type=MESH
        ).start()

    lo, hi = pl.ds(0, DH), pl.ds(DH, DH)

    def ag1(c):
        ss, rs = ag1_s.at[c % 2], ag1_r.at[c]
        res = []
        for d in (1, 2, 3):
            ref = xg.at[c, :, z, x, :, lo]
            res.append(rcopy(ref, ref, ss, rs, zx(0, d)))
            ref = xg.at[c, :, z, x, :, hi]
            res.append(rcopy(ref, ref, ss, rs, zx(d, 0)))
        return res, xg.at[c, :, 0, 0:3], ss, rs

    def ag2(c, t):
        ss, rs = ag2_s.at[c % 2, t], ag2_r.at[c, t]
        res = []
        for d in (1, 2, 3):
            ref = xg.at[c, t, z, :, :, lo]
            res.append(rcopy(ref, ref, ss, rs, zx(d, 0)))
            ref = xg.at[c, t, :, x, :, hi]
            res.append(rcopy(ref, ref, ss, rs, zx(0, d)))
        return res, xg.at[c, t, 0:3], ss, rs

    def core_swap(c, t):
        ss, rs = ce_s.at[c % 2, t], ce_r.at[c, t]
        return [rcopy(snd.at[t], crv.at[c, t], ss, rs, mate)], crv.at[c, t], ss, rs

    def rows(start, n):
        return pl.ds(pl.multiple_of(start, TB), n)

    a_keep, a_send = abit * 32, (1 - abit) * 32
    b_keep, b_send = 64 + bbit * 32, 64 + (1 - bbit) * 32
    a_own, a_send2 = a_keep + bbit * 16, a_keep + (1 - bbit) * 16
    b_own, b_send2 = b_keep + abit * 16, b_keep + (1 - abit) * 16

    def y_red1(c, t):
        ss, rs = y_s.at[c % 2, t, 0], y_r.at[c, t, 0]
        return [
            rcopy(s.at[c, t, rows(a_send, 32)], r1b.at[c, t, 0], ss, rs, pair_a),
            rcopy(s.at[c, t, rows(b_send, 32)], r1b.at[c, t, 1], ss, rs, pair_b),
        ], r1b.at[c, t], ss, rs

    def y_red2(c, t):
        ss, rs = y_s.at[c % 2, t, 1], y_r.at[c, t, 1]
        return [
            rcopy(s.at[c, t, rows(a_send2, 16)], r2b.at[c, t, 0], ss, rs, pair_b),
            rcopy(s.at[c, t, rows(b_send2, 16)], r2b.at[c, t, 1], ss, rs, pair_a),
        ], r2b.at[c, t], ss, rs

    def y_gat1(c, t):
        ss, rs = y_s.at[c % 2, t, 2], y_r.at[c, t, 2]
        ref_a = act.at[c, t, rows(core * HALF + a_own, 16)]
        ref_b = act.at[c, t, rows(core * HALF + b_own, 16)]
        return [rcopy(ref_a, ref_a, ss, rs, pair_b), rcopy(ref_b, ref_b, ss, rs, pair_a)], act.at[c, t, 0:32], ss, rs

    def y_gat2(c, t):
        ss, rs = y_s.at[c % 2, t, 3], y_r.at[c, t, 3]
        ref_a = act.at[c, t, rows(core * HALF + a_keep, 32)]
        ref_b = act.at[c, t, rows(core * HALF + b_keep, 32)]
        return [rcopy(ref_a, ref_a, ss, rs, pair_a), rcopy(ref_b, ref_b, ss, rs, pair_b)], act.at[c, t, 0:64], ss, rs

    def core_gat(c, t):
        ss, rs = gc_s.at[c % 2, t], gc_r.at[c, t]
        ref = act.at[c, t, rows(core * HALF, HALF)]
        return [rcopy(ref, ref, ss, rs, mate)], ref, ss, rs

    def rs1(c, t):
        ss, rs = rs1_s.at[c % 2, t], rs1_r.at[c, t]
        res = []
        for d in (1, 2, 3):
            src = part.at[c, t, :, (x + d) % 4, :, lo]
            res.append(rcopy(src, rab.at[c, t, 0, d - 1], ss, rs, zx(0, d)))
            src = part.at[c, t, (z + d) % 4, :, :, hi]
            res.append(rcopy(src, rab.at[c, t, 1, d - 1], ss, rs, zx(d, 0)))
        return res, rab.at[c, t], ss, rs

    def rs2(c):
        ss, rs = rs2_s.at[c % 2], rs2_r.at[c]
        res = []
        for d in (1, 2, 3):
            src = sab.at[c, 0, :, (z + d) % 4]
            res.append(rcopy(src, tab.at[c, 0, d - 1], ss, rs, zx(d, 0)))
            src = sab.at[c, 1, :, (x + d) % 4]
            res.append(rcopy(src, tab.at[c, 1, d - 1], ss, rs, zx(0, d)))
        return res, tab.at[c], ss, rs

    def start(stage):
        for send in stage[0]:
            send()

    def wait(stage):
        _, size, ss, rs = stage
        pltpu.make_async_copy(size, size, rs).wait()
        pltpu.make_async_copy(size, size, ss).wait()

    def half_of(c, t, which):
        return xg[c, t, pl.ds(2 * which, 2)].reshape(HALF, DL)

    def chunk_of(c, t):
        return xg[c, t].reshape(ROWS, DL)

    @pl.loop(0, CH + 9)
    def _(i):
        def stage(offset, fn):
            c = i - offset
            pl.when(jnp.logical_and(c >= 0, c < CH))(lambda: fn(c))

        def red2_stage(t):
            def run(c):
                wait(y_red1(c, t))
                for k, keep in ((0, a_keep), (1, b_keep)):
                    here = s.at[c, t, rows(keep, 32)]
                    here[...] = (here[...].astype(F32) + r1b[c, t, k].astype(F32)).astype(BF16)
                start(y_red2(c, t))

            return run

        def gelu_stage(c):
            wait(y_red2(c, 0))
            wait(y_red2(c, 1))
            for k, mine in ((0, a_own), (1, b_own)):
                total = s[c, :, rows(mine, 16)].astype(F32) + r2b[c, :, k].astype(F32)
                hidden = total[0] + b_in[...][None]
                half = 0.5 * (1.0 + lax.erf(hidden * 0.7071067811865476))
                slope = half + hidden * jnp.exp(-0.5 * hidden * hidden) * 0.3989422804014327
                at = rows(core * HALF + mine, 16)
                act[c, 0, at] = (hidden * half).astype(BF16)
                act[c, 1, at] = (total[1] * slope).astype(BF16)
            start(y_gat1(c, 0))
            start(y_gat1(c, 1))

        def gat2_stage(t):
            def run(c):
                wait(y_gat1(c, t))
                start(y_gat2(c, t))

            return run

        def core_gat_stage(t):
            def run(c):
                wait(y_gat2(c, t))
                start(core_gat(c, t))

            return run

        def ag1_stage(c):
            start(ag1(c))

        def ag2_stage(c):
            wait(ag1(c))
            start(ag2(c, 0))
            start(ag2(c, 1))

        def hidden_stage(t):
            def run(c):
                @pl.when(c == 0)
                def _():
                    loads[2 + t].wait()
                    loads[4 + t].wait()

                wait(ag2(c, t))
                lhs = jnp.concatenate([half_of(c, t, 1 - core), half_of(c, t, core)], axis=0)
                for n in range(0, FL, 512):
                    if t == 0:
                        r = dot(lhs, w_in[:, n:n + 512], (1, 0))
                    else:
                        r = dot(lhs, w_out[n:n + 512, :], (1, 1))
                    snd[t, :, n:n + 512] = r[:HALF].astype(BF16)
                    own[t, :, n:n + 512] = r[HALF:]
                start(core_swap(c, t))

            return run

        def out_stage(t):
            def run(c):
                wait(core_gat(c, t))
                for n in range(0, DL, 256):
                    if t == 0:
                        r = dot(act[c, 0], w_out[:, n:n + 256], (1, 0))
                    else:
                        r = dot(act[c, 1], w_in[n:n + 256, :], (1, 1))
                    part[c, t, :, :, :, n:n + 256] = r.astype(BF16).reshape(4, 4, TB, 256)
                start(rs1(c, t))

            return run

        def red1_stage(t):
            def run(c):
                wait(core_swap(c, t))
                s[c, t] = (own[t] + crv[c, t].astype(F32)).astype(BF16)
                start(y_red1(c, t))

            return run

        def rs2_stage(c):
            for t in (0, 1):
                wait(rs1(c, t))
                total = part[c, t, :, x, :, lo].astype(F32)
                for d in range(3):
                    total += rab[c, t, 0, d].astype(F32)
                sab[c, 0, t] = total.astype(BF16)
                total = part[c, t, z, :, :, hi].astype(F32)
                for d in range(3):
                    total += rab[c, t, 1, d].astype(F32)
                sab[c, 1, t] = total.astype(BF16)
            start(rs2(c))

        def final_stage(c):
            wait(rs2(c))
            for k, me, cols in ((0, z, lo), (1, x, hi)):
                total = sab[c, k, :, me].astype(F32)
                for d in range(3):
                    total += tab[c, k, d].astype(F32)
                out_o[c, :, cols] = (total[0] + b_out[cols][None]).astype(BF16)
                out_i[c, :, cols] = total[1].astype(BF16)

        def weight_stage(c):
            g_k = chunk_of(c, 1)
            for n in range(0, FL, 512):
                w2g[n:n + 512, :] += dot(act[c, 0, :, n:n + 512], g_k, (0, 0))
            x_k = chunk_of(c, 0)
            for n in range(0, FL, 512):
                w1g[:, n:n + 512] += dot(x_k, act[c, 1, :, n:n + 512], (0, 0))
            b1g[...] += jnp.sum(act[c, 1].astype(F32), axis=0, keepdims=True)
            b2g[...] += jnp.sum(g_k.astype(F32), axis=0, keepdims=True)

        def zero_stage(c):
            @pl.when(c == 0)
            def _():
                w1g[...] = jnp.zeros_like(w1g)
                w2g[...] = jnp.zeros_like(w2g)
                b1g[...] = jnp.zeros_like(b1g)
                b2g[...] = jnp.zeros_like(b2g)

        stage(6, gat2_stage(0))
        stage(4, red2_stage(0))
        stage(3, red1_stage(0))
        stage(5, gelu_stage)
        stage(6, gat2_stage(1))
        stage(4, red2_stage(1))
        stage(3, red1_stage(1))
        stage(7, core_gat_stage(0))
        stage(1, ag2_stage)
        stage(0, ag1_stage)
        stage(1, zero_stage)
        stage(2, hidden_stage(0))
        stage(7, core_gat_stage(1))
        stage(7, out_stage(0))
        stage(2, hidden_stage(1))
        stage(7, out_stage(1))
        stage(9, final_stage)
        stage(8, rs2_stage)
        stage(7, weight_stage)

    out_b1[...] = jnp.sum(b1g[...], axis=0)
    out_b2[...] = jnp.sum(b2g[...], axis=0)


def write_out(*refs):
    sems = refs[-1]
    copies = [pltpu.make_async_copy(refs[k], refs[k + 6], sems.at[k]) for k in range(6)]
    for cp in copies:
        cp.start()
    for cp in copies:
        cp.wait()


def shards(inputs, w_in, b_in, w_out, b_out, out_grad):
    any_spec = pl.BlockSpec(memory_space=pl.ANY)
    vmem_spec = pl.BlockSpec(memory_space=pltpu.VMEM)
    dma = pltpu.SemaphoreType.DMA
    outs = pl.pallas_call(
        body,
        out_shape=[
            pltpu.VMEM((CH, TB, DL), BF16),
            pltpu.VMEM((CH, TB, DL), BF16),
            pltpu.VMEM((DL, FL), F32),
            pltpu.VMEM((FL,), F32),
            pltpu.VMEM((FL, DL), F32),
            pltpu.VMEM((DL,), F32),
        ],
        in_specs=[any_spec] * 6,
        out_specs=[vmem_spec] * 6,
        scratch_shapes=[
            pltpu.VMEM((CH, 2, 4, 4, TB, DL), BF16),
            pltpu.VMEM((DL, FL), BF16),
            pltpu.VMEM((FL, DL), BF16),
            pltpu.VMEM((2, HALF, FL), BF16),
            pltpu.VMEM((CH, 2, HALF, FL), BF16),
            pltpu.VMEM((2, HALF, FL), F32),
            pltpu.VMEM((CH, 2, HALF, FL), BF16),
            pltpu.VMEM((CH, 2, 2, 32, FL), BF16),
            pltpu.VMEM((CH, 2, 2, 16, FL), BF16),
            pltpu.VMEM((CH, 2, ROWS, FL), BF16),
            pltpu.VMEM((CH, 2, 4, 4, TB, DL), BF16),
            pltpu.VMEM((CH, 2, 2, 3, 4, TB, DH), BF16),
            pltpu.VMEM((CH, 2, 2, 4, TB, DH), BF16),
            pltpu.VMEM((CH, 2, 3, 2, TB, DH), BF16),
            pltpu.VMEM((1, FL), F32),
            pltpu.VMEM((1, DL), F32),
            pltpu.VMEM((FL,), F32),
            pltpu.VMEM((DL,), F32),
            dma((6,)),
            dma((2,)), dma((CH,)), dma((2, 2)), dma((CH, 2)),
            dma((2, 2)), dma((CH, 2)),
            dma((2, 2, 4)), dma((CH, 2, 4)),
            dma((2, 2)), dma((CH, 2)),
            dma((2, 2)), dma((CH, 2)), dma((2,)), dma((CH,)),
        ],
        compiler_params=pltpu.CompilerParams(
            collective_id=0, has_side_effects=True, vmem_limit_bytes=48 * 2**20
        ),
        cost_estimate=pl.CostEstimate(flops=18 * 10**9, bytes_accessed=15 * 10**6, transcendentals=10**6),
        name="mlp",
    )(
        inputs.reshape(CH, TB, DL), out_grad.reshape(CH, TB, DL), w_in, w_out,
        b_in, b_out,
    )
    outs = pl.pallas_call(
        write_out,
        out_shape=[jax.ShapeDtypeStruct(o.shape, o.dtype) for o in outs],
        in_specs=[vmem_spec] * 6,
        out_specs=[any_spec] * 6,
        scratch_shapes=[dma((6,))],
        compiler_params=pltpu.CompilerParams(vmem_limit_bytes=2**20),
        name="write_out",
    )(*[pltpu.with_memory_space_constraint(o, pltpu.VMEM) for o in outs])
    output, input_grad, *grads = outs
    return output.reshape(CH * TB, DL), input_grad.reshape(CH * TB, DL), *grads


def solution(mesh):
    placed = (
        P("col", "row"),
        P("row", "col"),
        P("col"),
        P("col", "row"),
        P("row"),
        P("col", "row"),
    )
    return jax.shard_map(
        shards,
        mesh=mesh,
        in_specs=placed,
        out_specs=(
            P("col", "row"),
            P("col", "row"),
            P("row", "col"),
            P("col"),
            P("col", "row"),
            P("row"),
        ),
        check_vma=False,
    )
```

time: 121 us -> 110 us (0.909)
  Pallas kernels: 120 us -> 109 us
    pallas_call x1, Pallas kernels: 116 us -> 105 us  [shards(): pl.pallas_call(body, out_shape=[pltpu.VMEM((CH, TB, DL), BF16), pltpu.VME...]
where the time goes in v3:
time: 110 us
  Pallas kernels  109 us (99%)
    pallas_call x1, Pallas kernels, shards(): pl.pallas_call(body, out_shape=[pltpu.VMEM((CH, TB, DL), BF16), pltpu.VME...  105 us
    pallas_call x1, Pallas kernels, shards(): pl.pallas_call(write_out, out_shape=[jax.ShapeDtypeStruct(o.shape, o.dtyp...  3.88 us

profile of v3, /device:TPU:0, one launch (start us, length us, event | category | flops | bytes accessed | tf_op | source)
XLA Modules:
  0.0 110.0 jit_solution(3994874902780889571)
XLA Ops:
  0.6 105.5 %mlp.1 = (bf16[5,16,768]{2,1,0:T(8,128)(2,1)S(1)}, bf16[5,16,768]{2,1,0:T(8,128)(2,1)S(1)}, f32[768,1536]{1,0:T(8,128)S(1)}, f32[1536]{0:T(1024)S(1)}, f32[1536,768]{1,0:T(8,128)S(1)}, /*index=5*/f32[768]{0:T(1024)S(1)}) custom-call(bf16[5,16,768]{2,1,0:T(8,128)(2,1)} %bitcast.4, bf16[5,16,768]{2,1,0:T(8,128)(2,1)} %bitcast.5, bf16[768,1536]{1,0:T(8,128)(2,1)} %w_in_hbm.1, ...), custom_call_target="tpu_custom_call" | custom-call | flops 17999998976 | bytes 15000000 | tf_op jit(solution)/shard_map/mlp/pallas_call | solution.py:336
  106.1 3.9 %write_out.1 = (bf16[5,16,768]{2,1,0:T(8,128)(2,1)}, bf16[5,16,768]{2,1,0:T(8,128)(2,1)}, f32[768,1536]{1,0:T(8,128)}, f32[1536]{0:T(1024)}, f32[1536,768]{1,0:T(8,128)}, /*index=5*/f32[768]{0:T(1024)}) custom-call(bf16[5,16,768]{2,1,0:T(8,128)(2,1)S(1)} %get-tuple-element.18.refs_0_, bf16[5,16,768]{2,1,0:T(8,128)(2,1)S(1)} %get-tuple-element.19.refs_1_, ...), custom_call_target="tpu_custom_call" | custom-call | tf_op jit(solution)/shard_map/write_out/pallas_call | solution.py:383

commit v4 on v3

v4 whole, which is shorter than its diff:
```python
import jax
import jax.numpy as jnp
from jax import lax
from jax.experimental import pallas as pl
from jax.experimental.pallas import tpu as pltpu
from jax.sharding import PartitionSpec as P

MESH = pl.DeviceIdType.MESH
BF16 = jnp.bfloat16
F32 = jnp.float32

CH = 5
TB = 16
ROWS = 256
HALF = ROWS // 2
DL = 768
FL = 1536
DH = DL // 2


SCHEDULE = (
    ("ag1", 0, 0), ("ag1", 0, 1), ("ag2", 0, 0), ("ag2", 0, 1), ("ag1", 1, 0), ("ag1", 1, 1), ("hid", 0, 0),
    ("hid", 0, 1), ("red1", 0, 0), ("ag2", 1, 0), ("ag2", 1, 1), ("ag1", 2, 0), ("ag1", 2, 1), ("red1", 0, 1),
    ("red2", 0, 0), ("hid", 1, 0), ("red2", 0, 1), ("hid", 1, 1), ("red1", 1, 0), ("ag2", 2, 0), ("ag2", 2, 1),
    ("ag1", 3, 0), ("ag1", 3, 1), ("gelu", 0, 0), ("red1", 1, 1), ("red2", 1, 0), ("gat2", 0, 0), ("hid", 2, 0),
    ("gat2", 0, 1), ("hid", 2, 1), ("red2", 1, 1), ("red1", 2, 0), ("ag2", 3, 0), ("ag2", 3, 1), ("ag1", 4, 0),
    ("ag1", 4, 1), ("red1", 2, 1), ("cg", 0, 0), ("cg", 0, 1), ("out", 0, 0), ("gelu", 1, 0), ("hid", 3, 0),
    ("out", 0, 1), ("red2", 2, 0), ("wt", 0, 0), ("hid", 3, 1), ("red2", 2, 1), ("red1", 3, 0), ("ag2", 4, 0),
    ("ag2", 4, 1), ("gat2", 1, 0), ("gat2", 1, 1), ("red1", 3, 1), ("rs2", 0, 0), ("gelu", 2, 0), ("red2", 3, 0),
    ("hid", 4, 0), ("cg", 1, 0), ("hid", 4, 1), ("red1", 4, 0), ("fin", 0, 0), ("cg", 1, 1), ("out", 1, 0),
    ("red1", 4, 1), ("red2", 3, 1), ("out", 1, 1), ("wt", 1, 0), ("gat2", 2, 0), ("gat2", 2, 1), ("red2", 4, 0),
    ("rs2", 1, 0), ("red2", 4, 1), ("gelu", 3, 0), ("cg", 2, 0), ("fin", 1, 0), ("cg", 2, 1), ("out", 2, 0),
    ("gelu", 4, 0), ("out", 2, 1), ("gat2", 3, 0), ("wt", 2, 0), ("gat2", 3, 1), ("gat2", 4, 0), ("gat2", 4, 1),
    ("cg", 3, 0), ("rs2", 2, 0), ("cg", 3, 1), ("out", 3, 0), ("cg", 4, 0), ("out", 3, 1), ("wt", 3, 0), ("cg", 4, 1),
    ("out", 4, 0), ("fin", 2, 0), ("out", 4, 1), ("wt", 4, 0), ("rs2", 3, 0), ("rs2", 4, 0), ("fin", 3, 0),
    ("fin", 4, 0),
)


def dot(a, b, dims):
    return lax.dot_general(a, b, ((dims[:1], dims[1:]), ((), ())), preferred_element_type=F32)


def body(
    x_hbm, g_hbm, w_in_hbm, w_out_hbm, b_in_hbm, b_out_hbm,
    out_o, out_i, w1g, out_b1, w2g, out_b2,
    xg, w_in, w_out, snd, crv, own, s, r1b, r2b, act, part, rab, sab, tab, b1g, b2g, b_in, b_out,
    load_sem, send_sem, ce_s, ag1_r, ag2_r, ce_r, y_r, gc_r, rs1_r, rs2_r,
):
    row, col = lax.axis_index("row"), lax.axis_index("col")
    y, core = row // 2, row % 2
    z, x = col // 4, col % 4
    abit, bbit = ((y + 1) // 2) % 2, y // 2
    ya, yb = y + 1 - 2 * (y % 2), 3 - y
    pair_a, pair_b = (ya * 2 + core, col), (yb * 2 + core, col)
    mate = (y * 2 + 1 - core, col)

    def zx(dz, dx):
        return (row, ((z + dz) % 4) * 4 + (x + dx) % 4)

    loads = [
        pltpu.make_async_copy(x_hbm, xg.at[:, 0, z, x], load_sem.at[0]),
        pltpu.make_async_copy(g_hbm, xg.at[:, 1, z, x], load_sem.at[1]),
        pltpu.make_async_copy(w_in_hbm, w_in, load_sem.at[2]),
        pltpu.make_async_copy(w_out_hbm, w_out, load_sem.at[3]),
        pltpu.make_async_copy(b_in_hbm, b_in, load_sem.at[4]),
        pltpu.make_async_copy(b_out_hbm, b_out, load_sem.at[5]),
    ]
    for cp in loads:
        cp.start()

    barrier = pltpu.get_barrier_semaphore()
    peers = [pair_a, pair_b, mate] + [zx(0, d) for d in (1, 2, 3)] + [zx(d, 0) for d in (1, 2, 3)]
    for p in peers:
        pl.semaphore_signal(barrier, inc=1, device_id=p, device_id_type=MESH)
    pl.semaphore_wait(barrier, len(peers))
    loads[0].wait()
    loads[1].wait()

    def rcopy(src, dst, ss, rs, dev):
        return lambda: pltpu.make_async_remote_copy(
            src_ref=src, dst_ref=dst, send_sem=ss, recv_sem=rs, device_id=dev, device_id_type=MESH
        ).start()

    lo, hi = pl.ds(0, DH), pl.ds(DH, DH)

    def ag1(c, t):
        rs = ag1_r.at[c, t]
        res = []
        for d in (1, 2, 3):
            ref = xg.at[c, t, z, x, :, lo]
            res.append(rcopy(ref, ref, send_sem.at[0], rs, zx(0, d)))
            ref = xg.at[c, t, z, x, :, hi]
            res.append(rcopy(ref, ref, send_sem.at[0], rs, zx(d, 0)))
        return res, xg.at[c, t, 0, 0:3], rs

    def ag2(c, t):
        rs = ag2_r.at[c, t]
        res = []
        for d in (1, 2, 3):
            ref = xg.at[c, t, z, :, :, lo]
            res.append(rcopy(ref, ref, send_sem.at[1], rs, zx(d, 0)))
            ref = xg.at[c, t, :, x, :, hi]
            res.append(rcopy(ref, ref, send_sem.at[1], rs, zx(0, d)))
        return res, xg.at[c, t, 0:3], rs

    def core_swap(c, t):
        rs = ce_r.at[c, t]
        return [rcopy(snd.at[t], crv.at[c, t], ce_s.at[t], rs, mate)], crv.at[c, t], rs

    def rows(start, n):
        return pl.ds(pl.multiple_of(start, TB), n)

    a_keep, a_send = abit * 32, (1 - abit) * 32
    b_keep, b_send = 64 + bbit * 32, 64 + (1 - bbit) * 32
    a_own, a_send2 = a_keep + bbit * 16, a_keep + (1 - bbit) * 16
    b_own, b_send2 = b_keep + abit * 16, b_keep + (1 - abit) * 16

    def y_red1(c, t):
        ss, rs = send_sem.at[2], y_r.at[c, t, 0]
        return [
            rcopy(s.at[c, t, rows(a_send, 32)], r1b.at[c, t, 0], ss, rs, pair_a),
            rcopy(s.at[c, t, rows(b_send, 32)], r1b.at[c, t, 1], ss, rs, pair_b),
        ], r1b.at[c, t], rs

    def y_red2(c, t):
        ss, rs = send_sem.at[3], y_r.at[c, t, 1]
        return [
            rcopy(s.at[c, t, rows(a_send2, 16)], r2b.at[c, t, 0], ss, rs, pair_b),
            rcopy(s.at[c, t, rows(b_send2, 16)], r2b.at[c, t, 1], ss, rs, pair_a),
        ], r2b.at[c, t], rs

    def y_gat1(c, t):
        ss, rs = send_sem.at[4], y_r.at[c, t, 2]
        ref_a = act.at[c, t, rows(core * HALF + a_own, 16)]
        ref_b = act.at[c, t, rows(core * HALF + b_own, 16)]
        return [rcopy(ref_a, ref_a, ss, rs, pair_b), rcopy(ref_b, ref_b, ss, rs, pair_a)], act.at[c, t, 0:32], rs

    def y_gat2(c, t):
        ss, rs = send_sem.at[5], y_r.at[c, t, 3]
        ref_a = act.at[c, t, rows(core * HALF + a_keep, 32)]
        ref_b = act.at[c, t, rows(core * HALF + b_keep, 32)]
        return [rcopy(ref_a, ref_a, ss, rs, pair_a), rcopy(ref_b, ref_b, ss, rs, pair_b)], act.at[c, t, 0:64], rs

    def core_gat(c, t):
        rs = gc_r.at[c, t]
        ref = act.at[c, t, rows(core * HALF, HALF)]
        return [rcopy(ref, ref, send_sem.at[6], rs, mate)], act.at[c, t, 0:HALF], rs

    def rs1(c, t):
        ss, rs = send_sem.at[7], rs1_r.at[c, t]
        res = []
        for d in (1, 2, 3):
            src = part.at[c, t, :, (x + d) % 4, :, lo]
            res.append(rcopy(src, rab.at[c, t, 0, d - 1], ss, rs, zx(0, d)))
            src = part.at[c, t, (z + d) % 4, :, :, hi]
            res.append(rcopy(src, rab.at[c, t, 1, d - 1], ss, rs, zx(d, 0)))
        return res, rab.at[c, t], rs

    def rs2(c):
        ss, rs = send_sem.at[8], rs2_r.at[c]
        res = []
        for d in (1, 2, 3):
            src = sab.at[c, 0, :, (z + d) % 4]
            res.append(rcopy(src, tab.at[c, 0, d - 1], ss, rs, zx(d, 0)))
            src = sab.at[c, 1, :, (x + d) % 4]
            res.append(rcopy(src, tab.at[c, 1, d - 1], ss, rs, zx(0, d)))
        return res, tab.at[c], rs

    def start(stage):
        for send in stage[0]:
            send()

    def wait_bytes(size, sem):
        pltpu.make_async_copy(size, size, sem).wait()

    def wait(stage):
        wait_bytes(*stage[1:])

    def half_of(c, t, which):
        return xg[c, t, pl.ds(2 * which, 2)].reshape(HALF, DL)

    def chunk_of(c, t):
        return xg[c, t].reshape(ROWS, DL)

    def ag1_stage(c, t):
        start(ag1(c, t))

    def ag2_stage(c, t):
        wait(ag1(c, t))
        start(ag2(c, t))

    def hidden_stage(c, t):
        if c == 0:
            loads[2 + t].wait()
            loads[4 + t].wait()
        wait(ag2(c, t))
        lhs = jnp.concatenate([half_of(c, t, 1 - core), half_of(c, t, core)], axis=0)
        for n in range(0, FL, 512):
            if t == 0:
                r = dot(lhs, w_in[:, n:n + 512], (1, 0))
            else:
                r = dot(lhs, w_out[n:n + 512, :], (1, 1))
            snd[t, :, n:n + 512] = r[:HALF].astype(BF16)
            own[t, :, n:n + 512] = r[HALF:]
        start(core_swap(c, t))

    def red1_stage(c, t):
        wait(core_swap(c, t))
        wait_bytes(snd.at[t], ce_s.at[t])
        s[c, t] = (own[t] + crv[c, t].astype(F32)).astype(BF16)
        start(y_red1(c, t))

    def red2_stage(c, t):
        wait(y_red1(c, t))
        for k, keep in ((0, a_keep), (1, b_keep)):
            here = s.at[c, t, rows(keep, 32)]
            here[...] = (here[...].astype(F32) + r1b[c, t, k].astype(F32)).astype(BF16)
        start(y_red2(c, t))

    def gelu_stage(c, _):
        wait(y_red2(c, 0))
        wait(y_red2(c, 1))
        for k, mine in ((0, a_own), (1, b_own)):
            total = s[c, :, rows(mine, 16)].astype(F32) + r2b[c, :, k].astype(F32)
            hidden = total[0] + b_in[...][None]
            half = 0.5 * (1.0 + lax.erf(hidden * 0.7071067811865476))
            slope = half + hidden * jnp.exp(-0.5 * hidden * hidden) * 0.3989422804014327
            at = rows(core * HALF + mine, 16)
            act[c, 0, at] = (hidden * half).astype(BF16)
            act[c, 1, at] = (total[1] * slope).astype(BF16)
        start(y_gat1(c, 0))
        start(y_gat1(c, 1))

    def gat2_stage(c, t):
        wait(y_gat1(c, t))
        start(y_gat2(c, t))

    def core_gat_stage(c, t):
        wait(y_gat2(c, t))
        start(core_gat(c, t))

    def out_stage(c, t):
        wait(core_gat(c, t))
        for n in range(0, DL, 256):
            if t == 0:
                r = dot(act[c, 0], w_out[:, n:n + 256], (1, 0))
            else:
                r = dot(act[c, 1], w_in[n:n + 256, :], (1, 1))
            part[c, t, :, :, :, n:n + 256] = r.astype(BF16).reshape(4, 4, TB, 256)
        start(rs1(c, t))

    def rs2_stage(c, _):
        for t in (0, 1):
            wait(rs1(c, t))
            total = part[c, t, :, x, :, lo].astype(F32)
            for d in range(3):
                total += rab[c, t, 0, d].astype(F32)
            sab[c, 0, t] = total.astype(BF16)
            total = part[c, t, z, :, :, hi].astype(F32)
            for d in range(3):
                total += rab[c, t, 1, d].astype(F32)
            sab[c, 1, t] = total.astype(BF16)
        start(rs2(c))

    def final_stage(c, _):
        wait(rs2(c))
        for k, me, cols in ((0, z, lo), (1, x, hi)):
            total = sab[c, k, :, me].astype(F32)
            for d in range(3):
                total += tab[c, k, d].astype(F32)
            out_o[c, :, cols] = (total[0] + b_out[cols][None]).astype(BF16)
            out_i[c, :, cols] = total[1].astype(BF16)

    def weight_stage(c, _):
        def add(ref, at, value):
            ref[at] = value if c == 0 else ref[at] + value

        g_k = chunk_of(c, 1)
        for n in range(0, FL, 512):
            add(w2g, (slice(n, n + 512), slice(None)), dot(act[c, 0, :, n:n + 512], g_k, (0, 0)))
        x_k = chunk_of(c, 0)
        for n in range(0, FL, 512):
            add(w1g, (slice(None), slice(n, n + 512)), dot(x_k, act[c, 1, :, n:n + 512], (0, 0)))
        add(b1g, ..., jnp.sum(act[c, 1].astype(F32), axis=0, keepdims=True))
        add(b2g, ..., jnp.sum(g_k.astype(F32), axis=0, keepdims=True))

    stages = dict(
        ag1=ag1_stage, ag2=ag2_stage, hid=hidden_stage, red1=red1_stage, red2=red2_stage, gelu=gelu_stage,
        gat2=gat2_stage, cg=core_gat_stage, out=out_stage, rs2=rs2_stage, fin=final_stage, wt=weight_stage,
    )
    for name, c, t in SCHEDULE:
        stages[name](c, t)

    sent = (
        xg.at[:, :, 0, 0:3], xg.at[:, :, 0:3], r1b, r2b, act.at[:, :, 0:32], act.at[:, :, 0:64],
        act.at[:, :, 0:HALF], rab, tab,
    )
    for k, size in enumerate(sent):
        wait_bytes(size, send_sem.at[k])
    out_b1[...] = jnp.sum(b1g[...], axis=0)
    out_b2[...] = jnp.sum(b2g[...], axis=0)


def write_out(*refs):
    sems = refs[-1]
    copies = [pltpu.make_async_copy(refs[k], refs[k + 6], sems.at[k]) for k in range(6)]
    for cp in copies:
        cp.start()
    for cp in copies:
        cp.wait()


def shards(inputs, w_in, b_in, w_out, b_out, out_grad):
    any_spec = pl.BlockSpec(memory_space=pl.ANY)
    vmem_spec = pl.BlockSpec(memory_space=pltpu.VMEM)
    dma = pltpu.SemaphoreType.DMA
    outs = pl.pallas_call(
        body,
        out_shape=[
            pltpu.VMEM((CH, TB, DL), BF16),
            pltpu.VMEM((CH, TB, DL), BF16),
            pltpu.VMEM((DL, FL), F32),
            pltpu.VMEM((FL,), F32),
            pltpu.VMEM((FL, DL), F32),
            pltpu.VMEM((DL,), F32),
        ],
        in_specs=[any_spec] * 6,
        out_specs=[vmem_spec] * 6,
        scratch_shapes=[
            pltpu.VMEM((CH, 2, 4, 4, TB, DL), BF16),
            pltpu.VMEM((DL, FL), BF16),
            pltpu.VMEM((FL, DL), BF16),
            pltpu.VMEM((2, HALF, FL), BF16),
            pltpu.VMEM((CH, 2, HALF, FL), BF16),
            pltpu.VMEM((2, HALF, FL), F32),
            pltpu.VMEM((CH, 2, HALF, FL), BF16),
            pltpu.VMEM((CH, 2, 2, 32, FL), BF16),
            pltpu.VMEM((CH, 2, 2, 16, FL), BF16),
            pltpu.VMEM((CH, 2, ROWS, FL), BF16),
            pltpu.VMEM((CH, 2, 4, 4, TB, DL), BF16),
            pltpu.VMEM((CH, 2, 2, 3, 4, TB, DH), BF16),
            pltpu.VMEM((CH, 2, 2, 4, TB, DH), BF16),
            pltpu.VMEM((CH, 2, 3, 2, TB, DH), BF16),
            pltpu.VMEM((1, FL), F32),
            pltpu.VMEM((1, DL), F32),
            pltpu.VMEM((FL,), F32),
            pltpu.VMEM((DL,), F32),
            dma((6,)),
            dma((9,)), dma((2,)),
            dma((CH, 2)), dma((CH, 2)), dma((CH, 2)), dma((CH, 2, 4)), dma((CH, 2)), dma((CH, 2)), dma((CH,)),
        ],
        compiler_params=pltpu.CompilerParams(
            collective_id=0, has_side_effects=True, vmem_limit_bytes=48 * 2**20
        ),
        cost_estimate=pl.CostEstimate(flops=18 * 10**9, bytes_accessed=15 * 10**6, transcendentals=10**6),
        name="mlp",
    )(
        inputs.reshape(CH, TB, DL), out_grad.reshape(CH, TB, DL), w_in, w_out,
        b_in, b_out,
    )
    outs = pl.pallas_call(
        write_out,
        out_shape=[jax.ShapeDtypeStruct(o.shape, o.dtype) for o in outs],
        in_specs=[vmem_spec] * 6,
        out_specs=[any_spec] * 6,
        scratch_shapes=[dma((6,))],
        compiler_params=pltpu.CompilerParams(vmem_limit_bytes=2**20),
        name="write_out",
    )(*[pltpu.with_memory_space_constraint(o, pltpu.VMEM) for o in outs])
    output, input_grad, *grads = outs
    return output.reshape(CH * TB, DL), input_grad.reshape(CH * TB, DL), *grads


def solution(mesh):
    placed = (
        P("col", "row"),
        P("row", "col"),
        P("col"),
        P("col", "row"),
        P("row"),
        P("col", "row"),
    )
    return jax.shard_map(
        shards,
        mesh=mesh,
        in_specs=placed,
        out_specs=(
            P("col", "row"),
            P("col", "row"),
            P("row", "col"),
            P("col"),
            P("col", "row"),
            P("row"),
        ),
        check_vma=False,
    )
```

time: 110 us -> 107 us (0.973)
  Pallas kernels: 109 us -> 106 us
    pallas_call x1, Pallas kernels: 105 us -> 102 us  [shards(): pl.pallas_call(body, out_shape=[pltpu.VMEM((CH, TB, DL), BF16), pltpu.VME...]
where the time goes in v4:
time: 107 us
  Pallas kernels  106 us (99%)
    pallas_call x1, Pallas kernels, shards(): pl.pallas_call(body, out_shape=[pltpu.VMEM((CH, TB, DL), BF16), pltpu.VME...  102 us
    pallas_call x1, Pallas kernels, shards(): pl.pallas_call(write_out, out_shape=[jax.ShapeDtypeStruct(o.shape, o.dtyp...  3.88 us

profile of v4, /device:TPU:0, one launch (start us, length us, event | category | flops | bytes accessed | tf_op | source)
XLA Modules:
  0.0 106.8 jit_solution(11195932617655478179)
XLA Ops:
  0.6 102.1 %mlp.1 = (bf16[5,16,768]{2,1,0:T(8,128)(2,1)S(1)}, bf16[5,16,768]{2,1,0:T(8,128)(2,1)S(1)}, f32[768,1536]{1,0:T(8,128)S(1)}, f32[1536]{0:T(1024)S(1)}, f32[1536,768]{1,0:T(8,128)S(1)}, /*index=5*/f32[768]{0:T(1024)S(1)}) custom-call(bf16[5,16,768]{2,1,0:T(8,128)(2,1)} %bitcast.4, bf16[5,16,768]{2,1,0:T(8,128)(2,1)} %bitcast.5, bf16[768,1536]{1,0:T(8,128)(2,1)} %w_in_hbm.1, ...), custom_call_target="tpu_custom_call" | custom-call | flops 17999998976 | bytes 15000000 | tf_op jit(solution)/shard_map/mlp/pallas_call | solution.py:318
  102.8 3.9 %write_out.1 = (bf16[5,16,768]{2,1,0:T(8,128)(2,1)}, bf16[5,16,768]{2,1,0:T(8,128)(2,1)}, f32[768,1536]{1,0:T(8,128)}, f32[1536]{0:T(1024)}, f32[1536,768]{1,0:T(8,128)}, /*index=5*/f32[768]{0:T(1024)}) custom-call(bf16[5,16,768]{2,1,0:T(8,128)(2,1)S(1)} %get-tuple-element.18.refs_0_, bf16[5,16,768]{2,1,0:T(8,128)(2,1)S(1)} %get-tuple-element.19.refs_1_, ...), custom_call_target="tpu_custom_call" | custom-call | tf_op jit(solution)/shard_map/write_out/pallas_call | solution.py:362

commit v5 on v4

--- a/solution.py
+++ b/solution.py
@@ -19,21 +19,19 @@
 
 
 SCHEDULE = (
-    ("ag1", 0, 0), ("ag1", 0, 1), ("ag2", 0, 0), ("ag2", 0, 1), ("ag1", 1, 0), ("ag1", 1, 1), ("hid", 0, 0),
-    ("hid", 0, 1), ("red1", 0, 0), ("ag2", 1, 0), ("ag2", 1, 1), ("ag1", 2, 0), ("ag1", 2, 1), ("red1", 0, 1),
-    ("red2", 0, 0), ("hid", 1, 0), ("red2", 0, 1), ("hid", 1, 1), ("red1", 1, 0), ("ag2", 2, 0), ("ag2", 2, 1),
-    ("ag1", 3, 0), ("ag1", 3, 1), ("gelu", 0, 0), ("red1", 1, 1), ("red2", 1, 0), ("gat2", 0, 0), ("hid", 2, 0),
-    ("gat2", 0, 1), ("hid", 2, 1), ("red2", 1, 1), ("red1", 2, 0), ("ag2", 3, 0), ("ag2", 3, 1), ("ag1", 4, 0),
-    ("ag1", 4, 1), ("red1", 2, 1), ("cg", 0, 0), ("cg", 0, 1), ("out", 0, 0), ("gelu", 1, 0), ("hid", 3, 0),
-    ("out", 0, 1), ("red2", 2, 0), ("wt", 0, 0), ("hid", 3, 1), ("red2", 2, 1), ("red1", 3, 0), ("ag2", 4, 0),
-    ("ag2", 4, 1), ("gat2", 1, 0), ("gat2", 1, 1), ("red1", 3, 1), ("rs2", 0, 0), ("gelu", 2, 0), ("red2", 3, 0),
-    ("hid", 4, 0), ("cg", 1, 0), ("hid", 4, 1), ("red1", 4, 0), ("fin", 0, 0), ("cg", 1, 1), ("out", 1, 0),
-    ("red1", 4, 1), ("red2", 3, 1), ("out", 1, 1), ("wt", 1, 0), ("gat2", 2, 0), ("gat2", 2, 1), ("red2", 4, 0),
-    ("rs2", 1, 0), ("red2", 4, 1), ("gelu", 3, 0), ("cg", 2, 0), ("fin", 1, 0), ("cg", 2, 1), ("out", 2, 0),
-    ("gelu", 4, 0), ("out", 2, 1), ("gat2", 3, 0), ("wt", 2, 0), ("gat2", 3, 1), ("gat2", 4, 0), ("gat2", 4, 1),
-    ("cg", 3, 0), ("rs2", 2, 0), ("cg", 3, 1), ("out", 3, 0), ("cg", 4, 0), ("out", 3, 1), ("wt", 3, 0), ("cg", 4, 1),
-    ("out", 4, 0), ("fin", 2, 0), ("out", 4, 1), ("wt", 4, 0), ("rs2", 3, 0), ("rs2", 4, 0), ("fin", 3, 0),
-    ("fin", 4, 0),
+    ("ag1", 0, 0), ("ag1", 1, 0), ("ag1", 1, 1), ("ag1", 0, 1), ("ag2", 0, 0), ("ag2", 0, 1), ("ag2", 1, 0),
+    ("hid", 0, 0), ("ag1", 2, 0), ("hid", 0, 1), ("red1", 0, 0), ("ag1", 2, 1), ("ag2", 1, 1), ("red1", 0, 1),
+    ("hid", 1, 0), ("red2", 0, 0), ("ag2", 2, 0), ("ag1", 3, 0), ("ag2", 2, 1), ("red1", 1, 0), ("hid", 1, 1),
+    ("red2", 0, 1), ("red1", 1, 1), ("hid", 2, 0), ("ag1", 3, 1), ("ag1", 4, 0), ("gelu", 0, 2), ("hid", 2, 1),
+    ("ag2", 3, 0), ("ag1", 4, 1), ("red2", 1, 2), ("red1", 2, 2), ("gat2", 0, 2), ("hid", 3, 0), ("gelu", 1, 2),
+    ("ag2", 3, 1), ("hid", 3, 1), ("ag2", 4, 0), ("red2", 2, 2), ("cg", 0, 2), ("red1", 3, 2), ("ag2", 4, 1),
+    ("hid", 4, 0), ("gelu", 2, 2), ("gat2", 1, 2), ("hid", 4, 1), ("red1", 4, 2), ("cg", 1, 2), ("red2", 3, 2),
+    ("gat2", 2, 2), ("out", 0, 0), ("out", 1, 0), ("gelu", 3, 2), ("out", 0, 1), ("red2", 4, 2), ("wt", 0, 2),
+    ("cg", 2, 2), ("out", 1, 1), ("rs2", 0, 2), ("gat2", 3, 0), ("out", 2, 0), ("gelu", 4, 2), ("gat2", 3, 1),
+    ("wt", 1, 2), ("out", 2, 1), ("cg", 3, 0), ("rs2", 1, 2), ("gat2", 4, 0), ("out", 3, 0), ("cg", 3, 1),
+    ("gat2", 4, 1), ("rs2", 2, 2), ("out", 3, 1), ("cg", 4, 0), ("fin", 0, 2), ("outa", 4, 0), ("wt", 2, 2),
+    ("outb", 4, 0), ("fin", 1, 2), ("cg", 4, 1), ("outa", 4, 1), ("fin", 2, 2), ("outb", 4, 1), ("rs2", 3, 2),
+    ("wt", 3, 2), ("rs2", 4, 0), ("rs2", 4, 1), ("wt", 4, 2), ("fin", 3, 2), ("fin", 4, 0), ("fin", 4, 1),
 )
 
 
@@ -116,34 +114,47 @@
     a_own, a_send2 = a_keep + bbit * 16, a_keep + (1 - bbit) * 16
     b_own, b_send2 = b_keep + abit * 16, b_keep + (1 - abit) * 16
 
+    def pick(t):
+        return slice(None) if t == 2 else t
+
+    def parts(t):
+        return (0, 1) if t == 2 else (t,)
+
+    def sent_as(name, c, t):
+        return (2,) if (name, c, 2) in SCHEDULE else parts(t)
+
     def y_red1(c, t):
-        ss, rs = send_sem.at[2], y_r.at[c, t, 0]
+        ss, rs = send_sem.at[2], y_r.at[c, t % 2, 0]
+        t = pick(t)
         return [
             rcopy(s.at[c, t, rows(a_send, 32)], r1b.at[c, t, 0], ss, rs, pair_a),
             rcopy(s.at[c, t, rows(b_send, 32)], r1b.at[c, t, 1], ss, rs, pair_b),
         ], r1b.at[c, t], rs
 
     def y_red2(c, t):
-        ss, rs = send_sem.at[3], y_r.at[c, t, 1]
+        ss, rs = send_sem.at[3], y_r.at[c, t % 2, 1]
+        t = pick(t)
         return [
             rcopy(s.at[c, t, rows(a_send2, 16)], r2b.at[c, t, 0], ss, rs, pair_b),
             rcopy(s.at[c, t, rows(b_send2, 16)], r2b.at[c, t, 1], ss, rs, pair_a),
         ], r2b.at[c, t], rs
 
-    def y_gat1(c, t):
-        ss, rs = send_sem.at[4], y_r.at[c, t, 2]
-        ref_a = act.at[c, t, rows(core * HALF + a_own, 16)]
-        ref_b = act.at[c, t, rows(core * HALF + b_own, 16)]
-        return [rcopy(ref_a, ref_a, ss, rs, pair_b), rcopy(ref_b, ref_b, ss, rs, pair_a)], act.at[c, t, 0:32], rs
+    def y_gat1(c):
+        ss, rs = send_sem.at[4], y_r.at[c, 0, 2]
+        ref_a = act.at[c, :, rows(core * HALF + a_own, 16)]
+        ref_b = act.at[c, :, rows(core * HALF + b_own, 16)]
+        return [rcopy(ref_a, ref_a, ss, rs, pair_b), rcopy(ref_b, ref_b, ss, rs, pair_a)], act.at[c, :, 0:32], rs
 
     def y_gat2(c, t):
-        ss, rs = send_sem.at[5], y_r.at[c, t, 3]
+        ss, rs = send_sem.at[5], y_r.at[c, t % 2, 3]
+        t = pick(t)
         ref_a = act.at[c, t, rows(core * HALF + a_keep, 32)]
         ref_b = act.at[c, t, rows(core * HALF + b_keep, 32)]
         return [rcopy(ref_a, ref_a, ss, rs, pair_a), rcopy(ref_b, ref_b, ss, rs, pair_b)], act.at[c, t, 0:64], rs
 
     def core_gat(c, t):
-        rs = gc_r.at[c, t]
+        rs = gc_r.at[c, t % 2]
+        t = pick(t)
         ref = act.at[c, t, rows(core * HALF, HALF)]
         return [rcopy(ref, ref, send_sem.at[6], rs, mate)], act.at[c, t, 0:HALF], rs
 
@@ -157,15 +168,25 @@
             res.append(rcopy(src, rab.at[c, t, 1, d - 1], ss, rs, zx(d, 0)))
         return res, rab.at[c, t], rs
 
-    def rs2(c):
-        ss, rs = send_sem.at[8], rs2_r.at[c]
+    def rs1_half(c, t, which):
+        ss, rs = send_sem.at[7], rs1_r.at[c, t]
+        z_two = pl.ds(2 * which, 2)
+        for d in (1, 2, 3):
+            src = part.at[c, t, z_two, (x + d) % 4, :, lo]
+            rcopy(src, rab.at[c, t, 0, d - 1, z_two], ss, rs, zx(0, d))()
+            src = part.at[c, t, (z + d) % 4, :, :, hi]
+            pl.when((z + d) % 4 // 2 == which)(rcopy(src, rab.at[c, t, 1, d - 1], ss, rs, zx(d, 0)))
+
+    def rs2(c, t):
+        ss, rs = send_sem.at[8], rs2_r.at[c, t % 2]
+        t = pick(t)
         res = []
         for d in (1, 2, 3):
-            src = sab.at[c, 0, :, (z + d) % 4]
-            res.append(rcopy(src, tab.at[c, 0, d - 1], ss, rs, zx(d, 0)))
-            src = sab.at[c, 1, :, (x + d) % 4]
-            res.append(rcopy(src, tab.at[c, 1, d - 1], ss, rs, zx(0, d)))
-        return res, tab.at[c], rs
+            src = sab.at[c, 0, t, (z + d) % 4]
+            res.append(rcopy(src, tab.at[c, 0, d - 1, t], ss, rs, zx(d, 0)))
+            src = sab.at[c, 1, t, (x + d) % 4]
+            res.append(rcopy(src, tab.at[c, 1, d - 1, t], ss, rs, zx(0, d)))
+        return res, tab.at[c, :, :, t], rs
 
     def start(stage):
         for send in stage[0]:
@@ -206,21 +227,24 @@
         start(core_swap(c, t))
 
     def red1_stage(c, t):
-        wait(core_swap(c, t))
-        wait_bytes(snd.at[t], ce_s.at[t])
-        s[c, t] = (own[t] + crv[c, t].astype(F32)).astype(BF16)
+        for p in parts(t):
+            wait(core_swap(c, p))
+            wait_bytes(snd.at[p], ce_s.at[p])
+            s[c, p] = (own[p] + crv[c, p].astype(F32)).astype(BF16)
         start(y_red1(c, t))
 
     def red2_stage(c, t):
-        wait(y_red1(c, t))
-        for k, keep in ((0, a_keep), (1, b_keep)):
-            here = s.at[c, t, rows(keep, 32)]
-            here[...] = (here[...].astype(F32) + r1b[c, t, k].astype(F32)).astype(BF16)
+        for p in sent_as("red1", c, t):
+            wait(y_red1(c, p))
+        for p in parts(t):
+            for k, keep in ((0, a_keep), (1, b_keep)):
+                here = s.at[c, p, rows(keep, 32)]
+                here[...] = (here[...].astype(F32) + r1b[c, p, k].astype(F32)).astype(BF16)
         start(y_red2(c, t))
 
     def gelu_stage(c, _):
-        wait(y_red2(c, 0))
-        wait(y_red2(c, 1))
+        for p in sent_as("red2", c, 2):
+            wait(y_red2(c, p))
         for k, mine in ((0, a_own), (1, b_own)):
             total = s[c, :, rows(mine, 16)].astype(F32) + r2b[c, :, k].astype(F32)
             hidden = total[0] + b_in[...][None]
@@ -229,11 +253,11 @@
             at = rows(core * HALF + mine, 16)
             act[c, 0, at] = (hidden * half).astype(BF16)
             act[c, 1, at] = (total[1] * slope).astype(BF16)
-        start(y_gat1(c, 0))
-        start(y_gat1(c, 1))
+        start(y_gat1(c))
 
     def gat2_stage(c, t):
-        wait(y_gat1(c, t))
+        if t != 1:
+            wait(y_gat1(c))
         start(y_gat2(c, t))
 
     def core_gat_stage(c, t):
@@ -241,7 +265,10 @@
         start(core_gat(c, t))
 
     def out_stage(c, t):
-        wait(core_gat(c, t))
+        if t in sent_as("cg", c, t):
+            wait(core_gat(c, t))
+        elif t == 0:
+            wait(core_gat(c, 2))
         for n in range(0, DL, 256):
             if t == 0:
                 r = dot(act[c, 0], w_out[:, n:n + 256], (1, 0))
@@ -250,27 +277,50 @@
             part[c, t, :, :, :, n:n + 256] = r.astype(BF16).reshape(4, 4, TB, 256)
         start(rs1(c, t))
 
-    def rs2_stage(c, _):
-        for t in (0, 1):
-            wait(rs1(c, t))
-            total = part[c, t, :, x, :, lo].astype(F32)
+    def out_half(c, t, which):
+        at = rows(which * HALF, HALF)
+        for n in range(0, DL, 256):
+            if t == 0:
+                r = dot(act[c, 0, at], w_out[:, n:n + 256], (1, 0))
+            else:
+                r = dot(act[c, 1, at], w_in[n:n + 256, :], (1, 1))
+            part[c, t, pl.ds(2 * which, 2), :, :, n:n + 256] = r.astype(BF16).reshape(2, 4, TB, 256)
+        rs1_half(c, t, which)
+
+    def out_own_stage(c, t):
+        out_half(c, t, core)
+
+    def out_other_stage(c, t):
+        if t in sent_as("cg", c, t):
+            wait(core_gat(c, t))
+        elif t == 0:
+            wait(core_gat(c, 2))
+        out_half(c, t, 1 - core)
+
+    def rs2_stage(c, t):
+        for p in parts(t):
+            wait(rs1(c, p))
+            total = part[c, p, :, x, :, lo].astype(F32)
             for d in range(3):
-                total += rab[c, t, 0, d].astype(F32)
-            sab[c, 0, t] = total.astype(BF16)
-            total = part[c, t, z, :, :, hi].astype(F32)
+                total += rab[c, p, 0, d].astype(F32)
+            sab[c, 0, p] = total.astype(BF16)
+            total = part[c, p, z, :, :, hi].astype(F32)
             for d in range(3):
-                total += rab[c, t, 1, d].astype(F32)
-            sab[c, 1, t] = total.astype(BF16)
-        start(rs2(c))
-
-    def final_stage(c, _):
-        wait(rs2(c))
+                total += rab[c, p, 1, d].astype(F32)
+            sab[c, 1, p] = total.astype(BF16)
+        start(rs2(c, t))
+
+    def final_stage(c, t):
+        wait(rs2(c, t))
         for k, me, cols in ((0, z, lo), (1, x, hi)):
-            total = sab[c, k, :, me].astype(F32)
-            for d in range(3):
-                total += tab[c, k, d].astype(F32)
-            out_o[c, :, cols] = (total[0] + b_out[cols][None]).astype(BF16)
-            out_i[c, :, cols] = total[1].astype(BF16)
+            for p in parts(t):
+                total = sab[c, k, p, me].astype(F32)
+                for d in range(3):
+                    total += tab[c, k, d, p].astype(F32)
+                if p == 0:
+                    out_o[c, :, cols] = (total + b_out[cols][None]).astype(BF16)
+                else:
+                    out_i[c, :, cols] = total.astype(BF16)
 
     def weight_stage(c, _):
         def add(ref, at, value):
@@ -287,7 +337,8 @@
 
     stages = dict(
         ag1=ag1_stage, ag2=ag2_stage, hid=hidden_stage, red1=red1_stage, red2=red2_stage, gelu=gelu_stage,
-        gat2=gat2_stage, cg=core_gat_stage, out=out_stage, rs2=rs2_stage, fin=final_stage, wt=weight_stage,
+        gat2=gat2_stage, cg=core_gat_stage, out=out_stage,
+        outa=out_own_stage, outb=out_other_stage, rs2=rs2_stage, fin=final_stage, wt=weight_stage,
     )
     for name, c, t in SCHEDULE:
         stages[name](c, t)
@@ -348,7 +399,7 @@
             pltpu.VMEM((DL,), F32),
             dma((6,)),
             dma((9,)), dma((2,)),
-            dma((CH, 2)), dma((CH, 2)), dma((CH, 2)), dma((CH, 2, 4)), dma((CH, 2)), dma((CH, 2)), dma((CH,)),
+            dma((CH, 2)), dma((CH, 2)), dma((CH, 2)), dma((CH, 2, 4)), dma((CH, 2)), dma((CH, 2)), dma((CH, 2)),
         ],
         compiler_params=pltpu.CompilerParams(
             collective_id=0, has_side_effects=True, vmem_limit_bytes=48 * 2**20

time: 107 us -> 105 us (0.981)
  Pallas kernels: 106 us -> 104 us
    pallas_call x1, Pallas kernels: 102 us -> 99.9 us  [shards(): pl.pallas_call(body, out_shape=[pltpu.VMEM((CH, TB, DL), BF16), pltpu.VME...]
where the time goes in v5:
time: 105 us
  Pallas kernels  104 us (99%)
    pallas_call x1, Pallas kernels, shards(): pl.pallas_call(body, out_shape=[pltpu.VMEM((CH, TB, DL), BF16), pltpu.VME...  99.9 us
    pallas_call x1, Pallas kernels, shards(): pl.pallas_call(write_out, out_shape=[jax.ShapeDtypeStruct(o.shape, o.dtyp...  3.88 us

profile of v5, /device:TPU:0, one launch (start us, length us, event | category | flops | bytes accessed | tf_op | source)
XLA Modules:
  0.0 104.6 jit_solution(9725518844893825268)
XLA Ops:
  0.6 99.9 %mlp.1 = (bf16[5,16,768]{2,1,0:T(8,128)(2,1)S(1)}, bf16[5,16,768]{2,1,0:T(8,128)(2,1)S(1)}, f32[768,1536]{1,0:T(8,128)S(1)}, f32[1536]{0:T(1024)S(1)}, f32[1536,768]{1,0:T(8,128)S(1)}, /*index=5*/f32[768]{0:T(1024)S(1)}) custom-call(bf16[5,16,768]{2,1,0:T(8,128)(2,1)} %bitcast.4, bf16[5,16,768]{2,1,0:T(8,128)(2,1)} %bitcast.5, bf16[768,1536]{1,0:T(8,128)(2,1)} %w_in_hbm.1, ...), custom_call_target="tpu_custom_call" | custom-call | flops 17999998976 | bytes 15000000 | tf_op jit(solution)/shard_map/mlp/pallas_call | solution.py:369
  100.5 3.9 %write_out.1 = (bf16[5,16,768]{2,1,0:T(8,128)(2,1)}, bf16[5,16,768]{2,1,0:T(8,128)(2,1)}, f32[768,1536]{1,0:T(8,128)}, f32[1536]{0:T(1024)}, f32[1536,768]{1,0:T(8,128)}, /*index=5*/f32[768]{0:T(1024)}) custom-call(bf16[5,16,768]{2,1,0:T(8,128)(2,1)S(1)} %get-tuple-element.18.refs_0_, bf16[5,16,768]{2,1,0:T(8,128)(2,1)S(1)} %get-tuple-element.19.refs_1_, ...), custom_call_target="tpu_custom_call" | custom-call | tf_op jit(solution)/shard_map/write_out/pallas_call | solution.py:413

commit v6 on v5

--- a/solution.py
+++ b/solution.py
@@ -64,13 +64,12 @@
         pltpu.make_async_copy(b_in_hbm, b_in, load_sem.at[4]),
         pltpu.make_async_copy(b_out_hbm, b_out, load_sem.at[5]),
     ]
-    for cp in loads:
-        cp.start()
-
     barrier = pltpu.get_barrier_semaphore()
     peers = [pair_a, pair_b, mate] + [zx(0, d) for d in (1, 2, 3)] + [zx(d, 0) for d in (1, 2, 3)]
     for p in peers:
         pl.semaphore_signal(barrier, inc=1, device_id=p, device_id_type=MESH)
+    for cp in loads:
+        cp.start()
     pl.semaphore_wait(barrier, len(peers))
     loads[0].wait()
     loads[1].wait()
@@ -334,6 +333,9 @@
             add(w1g, (slice(None), slice(n, n + 512)), dot(x_k, act[c, 1, :, n:n + 512], (0, 0)))
         add(b1g, ..., jnp.sum(act[c, 1].astype(F32), axis=0, keepdims=True))
         add(b2g, ..., jnp.sum(g_k.astype(F32), axis=0, keepdims=True))
+        if c == CH - 1:
+            out_b1[...] = jnp.sum(b1g[...], axis=0)
+            out_b2[...] = jnp.sum(b2g[...], axis=0)
 
     stages = dict(
         ag1=ag1_stage, ag2=ag2_stage, hid=hidden_stage, red1=red1_stage, red2=red2_stage, gelu=gelu_stage,
@@ -349,8 +351,6 @@
     )
     for k, size in enumerate(sent):
         wait_bytes(size, send_sem.at[k])
-    out_b1[...] = jnp.sum(b1g[...], axis=0)
-    out_b2[...] = jnp.sum(b2g[...], axis=0)
 
 
 def write_out(*refs):

time: 105 us -> 105 us (level)
  no operation moved by 1% of the time
where the time goes in v6:
time: 105 us
  Pallas kernels  104 us (99%)
    pallas_call x1, Pallas kernels, shards(): pl.pallas_call(body, out_shape=[pltpu.VMEM((CH, TB, DL), BF16), pltpu.VME...  99.9 us
    pallas_call x1, Pallas kernels, shards(): pl.pallas_call(write_out, out_shape=[jax.ShapeDtypeStruct(o.shape, o.dtyp...  3.88 us

profile of v6, /device:TPU:0, one launch (start us, length us, event | category | flops | bytes accessed | tf_op | source)
XLA Modules:
  0.0 104.6 jit_solution(17590923582489595071)
XLA Ops:
  0.6 99.9 %mlp.1 = (bf16[5,16,768]{2,1,0:T(8,128)(2,1)S(1)}, bf16[5,16,768]{2,1,0:T(8,128)(2,1)S(1)}, f32[768,1536]{1,0:T(8,128)S(1)}, f32[1536]{0:T(1024)S(1)}, f32[1536,768]{1,0:T(8,128)S(1)}, /*index=5*/f32[768]{0:T(1024)S(1)}) custom-call(bf16[5,16,768]{2,1,0:T(8,128)(2,1)} %bitcast.4, bf16[5,16,768]{2,1,0:T(8,128)(2,1)} %bitcast.5, bf16[768,1536]{1,0:T(8,128)(2,1)} %w_in_hbm.1, ...), custom_call_target="tpu_custom_call" | custom-call | flops 17999998976 | bytes 15000000 | tf_op jit(solution)/shard_map/mlp/pallas_call | solution.py:369
  100.5 3.9 %write_out.1 = (bf16[5,16,768]{2,1,0:T(8,128)(2,1)}, bf16[5,16,768]{2,1,0:T(8,128)(2,1)}, f32[768,1536]{1,0:T(8,128)}, f32[1536]{0:T(1024)}, f32[1536,768]{1,0:T(8,128)}, /*index=5*/f32[768]{0:T(1024)}) custom-call(bf16[5,16,768]{2,1,0:T(8,128)(2,1)S(1)} %get-tuple-element.18.refs_0_, bf16[5,16,768]{2,1,0:T(8,128)(2,1)S(1)} %get-tuple-element.19.refs_1_, ...), custom_call_target="tpu_custom_call" | custom-call | tf_op jit(solution)/shard_map/write_out/pallas_call | solution.py:413
